TPU v7x, 32 devices: a whole 2x2x4 slice. The times are simulated.
32 devices in a mesh: cols: 4 (over y, core), rows: 8 (over z, x).
Axes of the slice: x: 2, y: 2, z: 4, core: 2. Of those that a mesh axis runs over, the one named last changes fastest.
Arguments:
- prior_trials: bfloat16 [256, 64, 1024], P('cols', 'rows'), may hold values from -12 to 12
- courant: bfloat16 [64, 1024], P('rows'), may hold values from 0.039794922 to 0.10986328
- diffusion: bfloat16 [64, 1024], P('rows'), may hold values from 0.1796875 to 0.21972656
- obs_cell: int32 [8, 8, 128], P('rows'), may hold values from 0 to 1023
- obs_count: int32 [8, 8], P('rows', 'cols'), may hold values from 1 to 128, as said below
- obs_value: float32 [8, 8, 128], P('rows', 'cols'), may hold values from -6 to 6
- error_kind: int32 [8, 8, 128], P('rows', 'cols'), may hold values from 0 to 3
- error_std: float32 [4], replicated, may hold values from 0.1 to 0.4
Outputs:
- analysis: bfloat16 [256, 64, 1024], P('cols', 'rows')
Inputs may be any that keep to these rules, and one draw needn't show every extreme that they name: `obs_count`: some patch has exactly 128 live slots in every draw.
All inputs are finite; a program needn't handle non-finite values.
Results may differ from a plain program's by a relative error of at most 0.0069.
Values may be sent and summed in bfloat16 or wider, within the bound.
No kernel may reach another device: no remote copies, remote signals or barrier semaphores. Data moves between devices by JAX's collectives and lax.ppermute only.
A program may use at most 64 MiB of HBM per device.

v0:
```python
import jax
import jax.numpy as jnp
from jax import lax
from jax.sharding import PartitionSpec as P

TILE_NORTH_SPAN = 8
TILE_EAST_SPAN = 128
FSTEPS = 4
NSIT = 6


highest = lax.Precision.HIGHEST


def extended(x, sides, width):
    for axis, dim in sides:
        count, length = (lax.axis_size(axis), x.shape[dim])
        up = [(i, (i + 1) % count) for i in range(count - 1)]
        down = [(j, i) for i, j in up]
        last = lax.slice_in_dim(x, length - width, length, axis=dim)
        initial = lax.slice_in_dim(x, 0, width, axis=dim)
        before = lax.ppermute(last, axis, up)
        after = lax.ppermute(initial, axis, down)
        x = jnp.concatenate([before, x, after], axis=dim)
    return x


def one_step(padded, speed_field, spread_field):
    centre = padded[:, 1:-1]
    upwind = padded[:, :-2]
    downwind = padded[:, 2:]
    west_side = jnp.pad(centre, ((0, 0), (0, 0), (1, 0)))[:, :, :-1]
    east_side = jnp.pad(centre, ((0, 0), (0, 0), (0, 1)))[:, :, 1:]
    return (
        centre
        - speed_field * (centre - upwind)
        + spread_field * (upwind + downwind + west_side + east_side - 4.0 * centre)
    )


def transform(obs_block, center_y, center_x):
    members = obs_block.shape[0] - 4
    values = obs_block[:members]
    observed = obs_block[members]
    inverse = obs_block[members + 1]
    coord_y = obs_block[members + 2]
    coord_x = obs_block[members + 3]
    average = jnp.mean(values, axis=0)
    spread_obs = values - average
    localized = inverse * jnp.exp(
        -0.5 * ((coord_y - center_y) / TILE_NORTH_SPAN) ** 2
        - 0.5 * ((coord_x - center_x) / TILE_EAST_SPAN) ** 2
    )
    weighted = spread_obs * localized
    factor = float(members - 1)
    identity = jnp.eye(members, dtype=jnp.float32)
    system = identity + jnp.dot(weighted, spread_obs.T, precision=highest) / factor
    frobenius = jnp.sqrt(jnp.sum(system * system))
    iterate = system / frobenius
    inverse_root = identity
    for iteration in range(NSIT):
        middle = 1.5 * identity - 0.5 * jnp.dot(inverse_root, iterate, precision=highest)
        iterate = jnp.dot(iterate, middle, precision=highest)
        inverse_root = jnp.dot(middle, inverse_root, precision=highest)
    weights_root = inverse_root / jnp.sqrt(frobenius)
    inverse_full = jnp.dot(weights_root, weights_root, precision=highest)
    mean_gain = (
        jnp.dot(
            inverse_full,
            jnp.dot(weighted, observed - average, precision=highest),
            precision=highest,
        )
        / factor
    )
    combined = weights_root + mean_gain[:, None]
    mixing = combined - jnp.mean(combined, axis=0, keepdims=True) + 1.0 / members
    return mixing.astype(jnp.bfloat16)


def on_device(
    prior_trials, courant, diffusion, obs_cell, obs_count, obs_value, error_kind, error_std
):
    tile_trials, mesh_north_extent, slab_width = prior_trials.shape
    members = tile_trials * lax.axis_size("cols")
    tile_strip = obs_cell.shape[1]
    own_count = obs_count.shape[1]
    slots = obs_cell.shape[2]
    col_index = lax.axis_index("cols")
    row_index = lax.axis_index("rows")
    stacked = jnp.concatenate([prior_trials, courant[None], diffusion[None]], axis=0)
    widened = extended(stacked, (("rows", 1),), FSTEPS)
    trial_surface = widened[:tile_trials].astype(jnp.float32)
    speed_field = widened[tile_trials].astype(jnp.float32)
    spread_field = widened[tile_trials + 1].astype(jnp.float32)
    for iteration in range(FSTEPS):
        speed_field = speed_field[1:-1]
        spread_field = spread_field[1:-1]
        trial_surface = one_step(trial_surface, speed_field, spread_field)
    propagated_surface = trial_surface.astype(jnp.bfloat16)
    own_cell = lax.dynamic_slice_in_dim(obs_cell, col_index * own_count, own_count, 1)[0]
    patch_ids = col_index * own_count + jnp.arange(own_count, dtype=jnp.int32)
    cell_y = row_index * TILE_NORTH_SPAN + own_cell // TILE_EAST_SPAN
    cell_x = patch_ids[:, None] * TILE_EAST_SPAN + own_cell % TILE_EAST_SPAN
    live_mask = jnp.arange(slots, dtype=jnp.int32)[None, :] < obs_count[0][:, None]
    inverse_table = 1.0 / (error_std * error_std)
    kinds = jnp.arange(error_std.shape[0], dtype=jnp.int32)
    looked = jnp.sum(jnp.where(error_kind[0][:, :, None] == kinds, inverse_table, 0.0), axis=-1)
    inverse = jnp.where(live_mask, looked, 0.0)
    partition_sequence = propagated_surface.reshape(
        tile_trials, mesh_north_extent, tile_strip, TILE_EAST_SPAN
    )
    patches = lax.all_to_all(partition_sequence, "cols", split_axis=2, concat_axis=0, tiled=True)
    flattened_position = (
        own_cell // TILE_EAST_SPAN * (own_count * TILE_EAST_SPAN)
        + jnp.arange(own_count, dtype=jnp.int32)[:, None] * TILE_EAST_SPAN
        + own_cell % TILE_EAST_SPAN
    )
    drawn_readings = jnp.take(
        patches.reshape(members, mesh_north_extent * own_count * TILE_EAST_SPAN),
        flattened_position,
        axis=1,
    )
    obs_block = jnp.concatenate(
        [
            drawn_readings.astype(jnp.float32),
            obs_value,
            inverse[None],
            cell_y.astype(jnp.float32)[None],
            cell_x.astype(jnp.float32)[None],
        ],
        axis=0,
    )[None]
    beside_all = extended(obs_block, (("cols", 2), ("rows", 0)), 1)
    groups = jnp.stack(
        [
            jnp.transpose(beside_all[:, :, offset : offset + 3, :], (1, 0, 2, 3)).reshape(
                members + 4, 9 * slots
            )
            for offset in range(own_count)
        ],
        axis=0,
    )
    center_y = jnp.full(
        (own_count,),
        row_index.astype(jnp.float32) * TILE_NORTH_SPAN + (TILE_NORTH_SPAN - 1) / 2.0,
        dtype=jnp.float32,
    )
    center_x = patch_ids.astype(jnp.float32) * TILE_EAST_SPAN + (TILE_EAST_SPAN - 1) / 2.0
    mixing = jax.vmap(transform)(groups, center_y, center_x)
    analysis = jnp.einsum(
        "jypx,pjk->kypx", patches, mixing, preferred_element_type=jnp.float32
    ).astype(jnp.bfloat16)
    returned = lax.all_to_all(analysis, "cols", split_axis=0, concat_axis=2, tiled=True)
    return returned.reshape(tile_trials, mesh_north_extent, slab_width)


def solution(mesh):
    placed = (
        P("cols", "rows", None),
        P("rows", None),
        P("rows", None),
        P("rows", None, None),
        P("rows", "cols"),
        P("rows", "cols", None),
        P("rows", "cols", None),
        P(),
    )
    return jax.shard_map(
        on_device, mesh=mesh, in_specs=placed, out_specs=P("cols", "rows", None), check_vma=False
    )
```

profile of v0, /device:TPU:11, one launch (start us, length us, event | category | flops | bytes accessed | tf_op | source)
XLA Modules:
  0.0 155.8 jit_solution(800821136934280011)
XLA Ops:
  2.0 3.3 %collective-permute-start = (bf16[66,4,1024]{2,0,1:T(8,128)(2,1)S(1)}, bf16[66,4,1024]{2,0,1:T(8,128)(2,1)S(1)}, u32[]{:S(2)}, u32[]{:S(2)}) collective-permute-start(bf16[66,4,1024]{2,0,1:T(8,128)(2,1)S(1)} %copy.46), channel_id=1, source_target_pairs={{0,1},{1,2},{2,3},{3,4},{4,5},{5,6},{6,7},{8,9},{9,10},{10,11},{11... | collective-permute-start | bytes 1622024 | tf_op jit(solution)/shard_map/ppermute | solution.py:22
  5.5 2.1 %collective-permute-start.1 = (bf16[66,4,1024]{2,0,1:T(8,128)(2,1)S(1)}, bf16[66,4,1024]{2,0,1:T(8,128)(2,1)S(1)}, u32[]{:S(2)}, u32[]{:S(2)}) collective-permute-start(bf16[66,4,1024]{2,0,1:T(8,128)(2,1)S(1)} %copy.47), channel_id=1, source_target_pairs={{1,0},{2,1},{3,2},{4,3},{5,4},{6,5},{7,6},{9,8},{10,9},{11,10},{12... | collective-permute-start | bytes 1622024 | tf_op jit(solution)/shard_map/ppermute | solution.py:23
  7.6 23.2 %collective-permute-done = bf16[66,4,1024]{2,0,1:T(8,128)(2,1)S(1)} collective-permute-done((bf16[66,4,1024]{2,0,1:T(8,128)(2,1)S(1)}, bf16[66,4,1024]{2,0,1:T(8,128)(2,1)S(1)}, u32[]{:S(2)}, u32[]{:S(2)}) %collective-permute-start) | collective-permute-done | bytes 540704 | tf_op jit(solution)/shard_map/ppermute | solution.py:22
  31.8 1.7 %pad_maximum_fusion = bf16[66,16,1024]{2,1,0:T(8,128)(2,1)S(1)} fusion(bf16[66,4,1024]{2,1,0:T(4,128)(2,1)S(1)} %copy.49, bf16[1,8,1024]{2,1,0:T(8,128)(2,1)S(1)} %bitcast.150, bf16[1,8,1024]{2,1,0:T(8,128)(2,1)S(1)} %bitcast.153, bf16[64,8,1024]{2,1,0:T(8,128)(2,1)S(1)} %copy-done, bf16[66,4,1024]{2,1,0:T(4,128)(2,1)S(1)} %copy.48), kind=kLoop, calls=%fused_computation.33 | loop fusion | flops 10813440 | bytes 4325376 | tf_op jit(solution)/shard_map/concatenate | solution.py:24
  35.1 2.9 %fusion.4 = f32[64,14,1024]{2,1,0:T(8,128)S(1)} fusion(f32[64,14,1024]{2,1,0:T(8,128)S(1)} %slice.211, f32[64,16,1024]{2,1,0:T(8,128)S(1)} %slice_convert_fusion, f32[14,1024]{1,0:T(8,128)S(1)} %get-tuple-element.25, f32[14,1024]{1,0:T(8,128)S(1)} %get-tuple-element.26), kind=kLoop, calls=%fused_computation.11 | loop fusion | flops 9175040 | bytes 14794752 | tf_op jit(solution)/shard_map/add | solution.py:35
  39.0 2.9 %fusion.9 = f32[64,12,1024]{2,1,0:T(8,128)S(1)} fusion(f32[64,12,1024]{2,1,0:T(8,128)S(1)} %slice.216, f32[64,14,1024]{2,1,0:T(8,128)S(1)} %fusion.4, f32[12,1024]{1,0:T(8,128)S(1)} %get-tuple-element.23, f32[12,1024]{1,0:T(8,128)S(1)} %get-tuple-element.24), kind=kLoop, calls=%fused_computation.16 | loop fusion | flops 7864320 | bytes 12681216 | tf_op jit(solution)/shard_map/add | solution.py:35
  42.9 2.9 %fusion.14 = f32[64,10,1024]{2,1,0:T(8,128)S(1)} fusion(f32[64,10,1024]{2,1,0:T(8,128)S(1)} %slice.221, f32[64,12,1024]{2,1,0:T(8,128)S(1)} %fusion.9, f32[10,1024]{1,0:T(8,128)S(1)} %get-tuple-element.21, f32[10,1024]{1,0:T(8,128)S(1)} %get-tuple-element.22), kind=kLoop, calls=%fused_computation.21 | loop fusion | flops 6553600 | bytes 10567680 | tf_op jit(solution)/shard_map/add | solution.py:35
  46.4 1.8 %fusion.43 = bf16[64,8,8,128]{3,1,2,0:T(8,128)(2,1)S(1)} fusion(f32[64,8,1024]{2,1,0:T(8,128)S(1)} %slice.226, f32[64,10,1024]{2,1,0:T(8,128)S(1)} %fusion.14, f32[8,1024]{1,0:T(8,128)S(1)} %get-tuple-element.27, f32[8,1024]{1,0:T(8,128)S(1)} %get-tuple-element.28), kind=kLoop, calls=%fused_computation.68 | loop fusion | flops 5767168 | bytes 7405568 | tf_op jit(solution)/shard_map/reshape | solution.py:109
  49.5 5.0 %all-to-all-start = ((bf16[64,8,8,128]{3,1,0,2:T(8,128)(2,1)}), bf16[64,8,8,128]{3,1,0,2:T(8,128)(2,1)S(1)}, u32[]{:S(2)}, u32[]{:S(2)}) async-start(bf16[64,8,8,128]{3,1,0,2:T(8,128)(2,1)} %copy.50), calls=%async_computation | async-start | bytes 2097152 | tf_op jit(solution)/shard_map/all_to_all | solution.py:112
  54.8 13.3 %all-to-all-done = bf16[64,8,8,128]{3,1,0,2:T(8,128)(2,1)S(1)} async-done(((bf16[64,8,8,128]{3,1,0,2:T(8,128)(2,1)}), bf16[64,8,8,128]{3,1,0,2:T(8,128)(2,1)S(1)}, u32[]{:S(2)}, u32[]{:S(2)}) %all-to-all-start) | async-done | bytes 1048608 | tf_op jit(solution)/shard_map/all_to_all | solution.py:112
  69.5 2.2 %reshape.296 = bf16[256,2048]{0,1:T(8,128)(2,1)} reshape(bf16[4,64,8,2,128]{1,0,4,3,2:T(4,128)(2,1)S(1)} %copy.65) | data formatting | bytes 2097152 | tf_op jit(solution)/shard_map/reshape | solution.py:119
  71.6 2.3 %gather_fusion = bf16[256,256]{1,0:T(8,128)(2,1)S(1)} fusion(bf16[256,2048]{0,1:T(8,128)(2,1)} %reshape.296, s32[1024]{0:T(1024)S(1)} %pad_clamp_fusion), kind=kCustom, calls=%fused_computation | custom fusion | bytes 263168 | tf_op jit(solution)/shard_map/jit(_take)/gather | solution.py:118
  74.6 2.7 %collective-permute-start.2 = (f32[1,260,1,128]{3,2,0,1:T(1,128)S(1)}, f32[1,260,1,128]{3,2,0,1:T(1,128)S(1)}, u32[]{:S(2)}, u32[]{:S(2)}) collective-permute-start(f32[1,260,1,128]{3,2,0,1:T(1,128)S(1)} %get-tuple-element.13), channel_id=1, source_target_pairs={{0,8},{8,16},{16,24},{1,9},{9,17},{17,25},{2,10},{10,18},{18,26},{... | collective-permute-start | bytes 399368 | tf_op jit(solution)/shard_map/ppermute | solution.py:22
  77.4 1.9 %collective-permute-start.3 = (f32[1,260,1,128]{3,2,0,1:T(1,128)S(1)}, f32[1,260,1,128]{3,2,0,1:T(1,128)S(1)}, u32[]{:S(2)}, u32[]{:S(2)}) collective-permute-start(f32[1,260,1,128]{3,2,0,1:T(1,128)S(1)} %get-tuple-element.14), channel_id=1, source_target_pairs={{8,0},{16,8},{24,16},{9,1},{17,9},{25,17},{10,2},{18,10},{26,18},{... | collective-permute-start | bytes 399368 | tf_op jit(solution)/shard_map/ppermute | solution.py:23
  79.3 4.4 %collective-permute-done.3 = f32[1,260,1,128]{3,2,0,1:T(1,128)S(1)} collective-permute-done((f32[1,260,1,128]{3,2,0,1:T(1,128)S(1)}, f32[1,260,1,128]{3,2,0,1:T(1,128)S(1)}, u32[]{:S(2)}, u32[]{:S(2)}) %collective-permute-start.3) | collective-permute-done | bytes 133152 | tf_op jit(solution)/shard_map/ppermute | solution.py:23
  84.9 3.6 %collective-permute-start.4 = (f32[1,260,4,128]{3,2,0,1:T(4,128)}, f32[1,260,4,128]{3,2,0,1:T(4,128)S(1)}, u32[]{:S(2)}, u32[]{:S(2)}) collective-permute-start(f32[1,260,4,128]{3,2,0,1:T(4,128)} %pad_maximum_fusion.3), channel_id=1, source_target_pairs={{0,1},{1,2},{2,3},{3,4},{4,5},{5,6},{6,7},{8,9},{9,10},{10,11},{11... | collective-permute-start | bytes 1597448 | tf_op jit(solution)/shard_map/ppermute | solution.py:22
  88.5 1.9 %collective-permute-start.5 = (f32[1,260,4,128]{3,2,0,1:T(4,128)}, f32[1,260,4,128]{3,2,0,1:T(4,128)S(1)}, u32[]{:S(2)}, u32[]{:S(2)}) collective-permute-start(f32[1,260,4,128]{3,2,0,1:T(4,128)} %pad_maximum_fusion.3), channel_id=1, source_target_pairs={{1,0},{2,1},{3,2},{4,3},{5,4},{6,5},{7,6},{9,8},{10,9},{11,10},{12... | collective-permute-start | bytes 1597448 | tf_op jit(solution)/shard_map/ppermute | solution.py:23
  91.7 17.9 %collective-permute-done.4 = f32[1,260,4,128]{3,2,0,1:T(4,128)S(1)} collective-permute-done((f32[1,260,4,128]{3,2,0,1:T(4,128)}, f32[1,260,4,128]{3,2,0,1:T(4,128)S(1)}, u32[]{:S(2)}, u32[]{:S(2)}) %collective-permute-start.4) | collective-permute-done | bytes 532512 | tf_op jit(solution)/shard_map/ppermute | solution.py:22
  110.2 1.8 %slice_bitcast_fusion = (f32[260,3,3,128]{3,2,1,0:T(4,128)}, f32[260,3,3,128]{3,2,1,0:T(4,128)S(1)}) fusion(f32[3,260,4,128]{3,2,0,1:T(4,128)S(1)} %pad_maximum_fusion.1), kind=kLoop, calls=%fused_computation.42 | loop fusion | bytes 4792320 | tf_op jit(solution)/shard_map/transpose | solution.py:136
  112.0 1.7 %stack_reshape.6 = f32[1,260,1152]{2,1,0:T(8,128)} reshape(f32[260,3,3,128]{3,2,1,0:T(4,128)S(1)} %get-tuple-element.10) | data formatting | bytes 2396160 | tf_op jit(solution)/shard_map/stack;reshape | solution.py:134
  115.1 2.9 %stack_reshape.7 = f32[1,260,1152]{2,1,0:T(8,128)} reshape(f32[260,3,3,128]{3,2,1,0:T(4,128)} %get-tuple-element.9) | data formatting | bytes 2396160 | tf_op jit(solution)/shard_map/stack;reshape | solution.py:134
  119.6 2.9 %multiply_reduce_fusion = (f32[2]{0:T(128)S(1)}, f32[2,256,256]{2,1,0:T(8,128)S(1)}) fusion(f32[2,260,1152]{2,1,0:T(8,128)S(1)} %constant_dynamic-update-slice_fusion.4, f32[2,1152]{1,0:T(2,128)S(1)} %get-tuple-element.16, f32[2,1152]{1,0:T(2,128)S(1)} %bitcast.154, f32[256,256]{1,0:T(8,128)S(1)} %fusion.50), kind=kOutput, calls=%fused_computation.71 | convolution fusion | flops 1814233088 | bytes 5532680 | tf_op jit(solution)/shard_map/vmap()/dot_general | solution.py:57
  132.3 2.2 %fusion.15 = f32[2,1,256]{2,1,0:T(1,128)S(1)} fusion(f32[2,260,1152]{2,1,0:T(8,128)S(1)} %constant_dynamic-update-slice_fusion.4, f32[2,1152]{1,0:T(2,128)S(1)} %bitcast.155, f32[2,1152]{1,0:T(2,128)S(1)} %get-tuple-element.16, f32[2,1152,1]{1,0,2:T(2,128)S(1)} %get-tuple-element.15), kind=kOutput, calls=%fused_computation.25 | convolution fusion | flops 8257536 | bytes 2388992 | tf_op jit(solution)/shard_map/vmap()/dot_general | solution.py:70
  138.5 16.0 %all_to_all.33 = bf16[256,8,2,128]{3,1,2,0:T(8,128)(2,1)S(1)} all-to-all(bf16[256,8,2,128]{3,1,2,0:T(8,128)(2,1)S(1)} %copy.57), channel_id=1, replica_groups=mesh['cols'=4,'rows'=8] {'cols'}, dimensions={0} | all-to-all | bytes 2097152 | tf_op jit(solution)/shard_map/all_to_all | solution.py:153
  (92 shorter events, 31.5 us)
Async XLA Ops:
  1.8 29.9 %copy-start = (bf16[64,8,1024]{2,1,0:T(8,128)(2,1)S(1)}, bf16[64,8,1024]{2,1,0:T(8,128)(2,1)}, u32[]{:S(2)}) copy-start(bf16[64,8,1024]{2,1,0:T(8,128)(2,1)} %param.8) | copy-start | bytes 3145732
  1.8 29.9 %copy-start.2 = (bf16[8,1024]{1,0:T(8,128)(2,1)S(1)}, bf16[8,1024]{1,0:T(8,128)(2,1)}, u32[]{:S(2)}) copy-start(bf16[8,1024]{1,0:T(8,128)(2,1)} %param.10) | copy-start | bytes 49156
  1.8 29.9 %copy-start.3 = (bf16[8,1024]{1,0:T(8,128)(2,1)S(1)}, bf16[8,1024]{1,0:T(8,128)(2,1)}, u32[]{:S(2)}) copy-start(bf16[8,1024]{1,0:T(8,128)(2,1)} %param.9) | copy-start | bytes 49156
  2.0 28.9 %collective-permute-start = (bf16[66,4,1024]{2,0,1:T(8,128)(2,1)S(1)}, bf16[66,4,1024]{2,0,1:T(8,128)(2,1)S(1)}, u32[]{:S(2)}, u32[]{:S(2)}) collective-permute-start(bf16[66,4,1024]{2,0,1:T(8,128)(2,1)S(1)} %copy.46), channel_id=1, source_target_pairs={{0,1},{1,2},{2,3},{3,4},{4,5},{5,6},{6,7},{8,9},{9,10},{10,11},{11... | collective-permute-start | bytes 1622024 | tf_op jit(solution)/shard_map/ppermute | solution.py:22
  5.5 25.8 %collective-permute-start.1 = (bf16[66,4,1024]{2,0,1:T(8,128)(2,1)S(1)}, bf16[66,4,1024]{2,0,1:T(8,128)(2,1)S(1)}, u32[]{:S(2)}, u32[]{:S(2)}) collective-permute-start(bf16[66,4,1024]{2,0,1:T(8,128)(2,1)S(1)} %copy.47), channel_id=1, source_target_pairs={{1,0},{2,1},{3,2},{4,3},{5,4},{6,5},{7,6},{9,8},{10,9},{11,10},{12... | collective-permute-start | bytes 1622024 | tf_op jit(solution)/shard_map/ppermute | solution.py:23
  48.3 6.2 %copy-start.4 = (s32[1,8,128]{2,1,0:T(8,128)S(1)}, s32[1,8,128]{2,1,0:T(8,128)}, u32[]{:S(2)}) copy-start(s32[1,8,128]{2,1,0:T(8,128)} %param.11) | copy-start | bytes 12292
  48.3 6.3 %copy-start.8 = (f32[4]{0:T(128)S(1)}, f32[4]{0:T(128)}, u32[]{:S(2)}) copy-start(f32[4]{0:T(128)} %param.15) | copy-start | bytes 52
  48.3 6.3 %copy-start.5 = (s32[1,2,128]{2,1,0:T(2,128)S(1)}, s32[1,2,128]{2,1,0:T(2,128)}, u32[]{:S(2)}) copy-start(s32[1,2,128]{2,1,0:T(2,128)} %param.14) | copy-start | bytes 3076
  49.5 18.6 %all-to-all-start = ((bf16[64,8,8,128]{3,1,0,2:T(8,128)(2,1)}), bf16[64,8,8,128]{3,1,0,2:T(8,128)(2,1)S(1)}, u32[]{:S(2)}, u32[]{:S(2)}) async-start(bf16[64,8,8,128]{3,1,0,2:T(8,128)(2,1)} %copy.50), calls=%async_computation | async-start | bytes 2097152 | tf_op jit(solution)/shard_map/all_to_all | solution.py:112
  69.5 4.8 %copy-start.6 = (f32[1,2,128]{2,1,0:T(2,128)S(1)}, f32[1,2,128]{2,1,0:T(2,128)}, u32[]{:S(2)}) copy-start(f32[1,2,128]{2,1,0:T(2,128)} %param.13) | copy-start | bytes 3076
  69.5 4.8 %copy-start.7 = (s32[1,2]{1,0:T(1,128)S(1)}, s32[1,2]{1,0:T(1,128)}, u32[]{:S(2)}) copy-start(s32[1,2]{1,0:T(1,128)} %param.12) | copy-start | bytes 28
  74.6 4.7 %collective-permute-start.2 = (f32[1,260,1,128]{3,2,0,1:T(1,128)S(1)}, f32[1,260,1,128]{3,2,0,1:T(1,128)S(1)}, u32[]{:S(2)}, u32[]{:S(2)}) collective-permute-start(f32[1,260,1,128]{3,2,0,1:T(1,128)S(1)} %get-tuple-element.13), channel_id=1, source_target_pairs={{0,8},{8,16},{16,24},{1,9},{9,17},{17,25},{2,10},{10,18},{18,26},{... | collective-permute-start | bytes 399368 | tf_op jit(solution)/shard_map/ppermute | solution.py:22
  77.4 6.3 %collective-permute-start.3 = (f32[1,260,1,128]{3,2,0,1:T(1,128)S(1)}, f32[1,260,1,128]{3,2,0,1:T(1,128)S(1)}, u32[]{:S(2)}, u32[]{:S(2)}) collective-permute-start(f32[1,260,1,128]{3,2,0,1:T(1,128)S(1)} %get-tuple-element.14), channel_id=1, source_target_pairs={{8,0},{16,8},{24,16},{9,1},{17,9},{25,17},{10,2},{18,10},{26,18},{... | collective-permute-start | bytes 399368 | tf_op jit(solution)/shard_map/ppermute | solution.py:23
  84.9 24.7 %collective-permute-start.4 = (f32[1,260,4,128]{3,2,0,1:T(4,128)}, f32[1,260,4,128]{3,2,0,1:T(4,128)S(1)}, u32[]{:S(2)}, u32[]{:S(2)}) collective-permute-start(f32[1,260,4,128]{3,2,0,1:T(4,128)} %pad_maximum_fusion.3), channel_id=1, source_target_pairs={{0,1},{1,2},{2,3},{3,4},{4,5},{5,6},{6,7},{8,9},{9,10},{10,11},{11... | collective-permute-start | bytes 1597448 | tf_op jit(solution)/shard_map/ppermute | solution.py:22
  88.5 21.1 %collective-permute-start.5 = (f32[1,260,4,128]{3,2,0,1:T(4,128)}, f32[1,260,4,128]{3,2,0,1:T(4,128)S(1)}, u32[]{:S(2)}, u32[]{:S(2)}) collective-permute-start(f32[1,260,4,128]{3,2,0,1:T(4,128)} %pad_maximum_fusion.3), channel_id=1, source_target_pairs={{1,0},{2,1},{3,2},{4,3},{5,4},{6,5},{7,6},{9,8},{10,9},{11,10},{12... | collective-permute-start | bytes 1597448 | tf_op jit(solution)/shard_map/ppermute | solution.py:23
  135.2 2.1 %copy-start.1 = (bf16[4,64,8,2,128]{4,1,0,2,3:T(8,128)(2,1)S(1)}, bf16[4,64,8,2,128]{4,1,0,2,3:T(8,128)(2,1)}, u32[]{:S(2)}) copy-start(bf16[4,64,8,2,128]{4,1,0,2,3:T(8,128)(2,1)} %copy.55) | copy-start | bytes 3145732
where the time goes:
time: 159 us; the launch traced here: 156 us
  waiting for transfers between devices  58.8 us (37%)
  local copies, waits for them, and re-layouts  24.9 us (16%)
  starting transfers between devices  20.7 us (13%)
  matrix products  17.9 us (11%)
  other arithmetic  17 us (11%)
  blocking collectives  16 us (10%)
    ppermute x3, waiting for transfers between devices, extended(): before = lax.ppermute(last, axis, up)  41.1 us
    all_to_all x1, blocking collectives, on_device(): lax.all_to_all(analysis, 'cols', split_axis=0, concat_axis=2, tiled=True)  16 us
    all_to_all x1, waiting for transfers between devices, on_device(): lax.all_to_all(partition_sequence, 'cols', split_axis=2, concat_axis=0, t...  13.3 us
    ppermute x3, starting transfers between devices, extended(): before = lax.ppermute(last, axis, up)  9.68 us
    add x3, other arithmetic, one_step(): centre - speed_field * (centre - upwind)  8.74 us
    another operation x3, local copies, waits for them, and re-layouts, on_device(): jnp.stack([jnp.transpose(beside_all[:, :, offset:offset + 3, :], (1, 0, 2...  5.97 us
    ppermute x3, starting transfers between devices, extended(): after = lax.ppermute(initial, axis, down)  5.95 us
    all_to_all x1, starting transfers between devices, on_device(): lax.all_to_all(partition_sequence, 'cols', split_axis=2, concat_axis=0, t...  5.03 us
  transfers between devices with their start and end apart: 7, of which 4 were waited for; matrix products, arithmetic and copies ran while one was open for 1% of the time, Pallas kernels for 0%

commit v1 on v0

v1 whole, which is shorter than its diff:
```python
import functools
import jax
import jax.numpy as jnp
from jax import lax
from jax.experimental import pallas as pl
from jax.experimental.pallas import tpu as pltpu
from jax.sharding import PartitionSpec as P

ROWS = 8
LANES = 128
FSTEPS = 4
NSIT = 6
BLOCK = 16
LIMIT = 56 * 1024 * 1024
f32 = jnp.float32
bf16 = jnp.bfloat16

vmem = functools.partial(pl.BlockSpec, memory_space=pltpu.VMEM)
smem = functools.partial(pl.BlockSpec, memory_space=pltpu.SMEM)


def call(kernel, outs, scratch, flops, moved, args, specs):
    return pl.pallas_call(
        kernel,
        out_shape=outs,
        in_specs=specs,
        out_specs=[vmem() for _ in outs],
        scratch_shapes=scratch,
        compiler_params=pltpu.CompilerParams(vmem_limit_bytes=LIMIT),
        cost_estimate=pl.CostEstimate(flops=flops, bytes_accessed=moved, transcendentals=0),
    )(*args)


def forecast_kernel(first, offset, m, groups, me_ref, own_ref, up_ref, down_ref, *rest):
    if first:
        speed_ref, spread_ref, cell_ref = rest[:3]
        rest = rest[3:]
        coef_ref, sample_ref = rest[:2]
        rest = rest[2:]
    else:
        coef_ref, cell_ref, sample_ref = rest[:3]
        rest = rest[3:]
    parts = rest[:groups]
    even, odd = rest[groups:]
    width = own_ref.shape[2]
    tiles = width // LANES
    span = width // groups
    total = ROWS + 2 * FSTEPS
    if first:
        base = FSTEPS * m
        up_c = up_ref[base : base + BLOCK, :].astype(f32)
        down_c = down_ref[base : base + BLOCK, :].astype(f32)
        speed = jnp.concatenate(
            [up_c[:FSTEPS], speed_ref[...].astype(f32), down_c[:FSTEPS]], axis=0
        )
        spread = jnp.concatenate(
            [up_c[FSTEPS : 2 * FSTEPS], spread_ref[...].astype(f32), down_c[FSTEPS : 2 * FSTEPS]],
            axis=0,
        )
        coef_ref[0] = 1.0 - speed - 4.0 * spread
        coef_ref[1] = speed + spread
        coef_ref[2] = spread
    me = me_ref[0]
    lane = lax.broadcasted_iota(jnp.int32, (8, LANES), 1)
    leftmost = lane == 0
    rightmost = lane == LANES - 1

    def block(i, carry):
        start = pl.multiple_of(i * BLOCK, BLOCK)
        for r in range(FSTEPS):
            at = pl.multiple_of(r * m + start, BLOCK)
            even[r] = up_ref[pl.ds(at, BLOCK), :].astype(f32)
            even[r + FSTEPS + ROWS] = down_ref[pl.ds(at, BLOCK), :].astype(f32)
        for r in range(ROWS):
            even[r + FSTEPS] = own_ref[
                r, pl.ds(pl.multiple_of(offset + start, BLOCK), BLOCK), :
            ].astype(f32)
        source, target = even, odd
        for step in range(1, FSTEPS + 1):
            for half in range(0, BLOCK, 8):

                def row(r):
                    return [
                        source[r, half : half + 8, t * LANES : (t + 1) * LANES]
                        for t in range(tiles)
                    ]

                above, centre = row(step - 1), row(step)
                for r in range(step, total - step):
                    below = row(r + 1)
                    right = [pltpu.roll(c, 1, 1) for c in centre]
                    left = [pltpu.roll(c, LANES - 1, 1) for c in centre]
                    for t in range(tiles):
                        cut = slice(t * LANES, (t + 1) * LANES)
                        west = jnp.where(leftmost, right[t - 1] if t else 0.0, right[t])
                        east = jnp.where(
                            rightmost, left[t + 1] if t + 1 < tiles else 0.0, left[t]
                        )
                        target[r, half : half + 8, cut] = (
                            coef_ref[0, r : r + 1, cut] * centre[t]
                            + coef_ref[1, r : r + 1, cut] * above[t]
                            + coef_ref[2, r : r + 1, cut] * (below[t] + (west + east))
                        )
                    above, centre = centre, below
            source, target = target, source
        for t in range(tiles):
            cell = cell_ref[t : t + 1, :]
            at_row = jnp.broadcast_to(cell // LANES, (8, LANES))
            at_lane = jnp.broadcast_to(cell % LANES, (8, LANES))
            halves = []
            for half in range(0, BLOCK, 8):
                taken = jnp.zeros((8, LANES), f32)
                for y in range(ROWS):
                    values = source[
                        y + FSTEPS, half : half + 8, t * LANES : (t + 1) * LANES
                    ]
                    picked = jnp.take_along_axis(
                        values, at_lane, axis=1, mode="promise_in_bounds"
                    )
                    taken = jnp.where(at_row == y, picked, taken)
                halves.append(taken)
            sample_ref[pl.ds(start, BLOCK), t * LANES : (t + 1) * LANES] = jnp.concatenate(
                halves, axis=0
            ).astype(bf16)
        for d in range(groups):
            column = pl.multiple_of((me ^ d) * span, LANES)
            for y in range(ROWS):
                parts[d][y, pl.ds(start, BLOCK), :] = source[
                    y + FSTEPS, :, pl.ds(column, span)
                ].astype(bf16)
        return carry

    lax.fori_loop(0, m // BLOCK, block, 0)


def forecast(first, offset, m, groups, me, own, up, down, extra, cell):
    width = own.shape[2]
    total = ROWS + 2 * FSTEPS
    outs = []
    if first:
        outs.append(jax.ShapeDtypeStruct((3, total, width), f32))
    outs.append(jax.ShapeDtypeStruct((m, width), bf16))
    outs += [jax.ShapeDtypeStruct((ROWS, m, width // groups), bf16) for _ in range(groups)]
    args = (me, own, up, down) + tuple(extra) + (cell,)
    scratch = [pltpu.VMEM((total, BLOCK, width), f32)] * 2
    return call(
        functools.partial(forecast_kernel, first, offset, m, groups),
        outs,
        scratch,
        44 * m * width * 16,
        m * width * 2 * 30,
        args,
        [smem()] + [vmem()] * (len(args) - 1),
    )


def spread_kernel(groups, m, me_ref, up_ref, own_ref, down_ref, *rest):
    parts, padded = rest[:groups], rest[groups]
    width = own_ref.shape[1]
    span = width // groups
    me = me_ref[0]
    blank = jnp.zeros((m, LANES), bf16)
    for i, ref in enumerate((up_ref, own_ref, down_ref)):
        padded[i, :, :LANES] = blank
        padded[i, :, LANES + width :] = blank
        padded[i, :, LANES : LANES + width] = ref[...]
    for d in range(groups):
        column = pl.multiple_of((me ^ d) * span, LANES)
        for i in range(3):
            parts[d][i] = padded[i, :, pl.ds(column, span + 2 * LANES)]


def spread_samples(groups, me, up, own, down):
    m, width = own.shape
    wide = width // groups + 2 * LANES
    return call(
        functools.partial(spread_kernel, groups, m),
        [jax.ShapeDtypeStruct((3, m, wide), bf16) for _ in range(groups)],
        [pltpu.VMEM((3, m, width + 2 * LANES), bf16)],
        0,
        m * width * 12,
        (me, up, own, down),
        [smem()] + [vmem()] * 3,
    )


def product(a, b):
    return jnp.dot(a, b, preferred_element_type=f32)


def halves_of(a):
    high = a.astype(bf16)
    return high, (a - high.astype(f32)).astype(bf16)


def wide_product(a, b):
    return product(a[0], b[0]) + (product(a[0], b[1]) + product(a[1], b[0]))


def transform_kernel(groups, chunks, left_ref, mid_ref, right_ref, *rest):
    count = groups * len(chunks)
    sample_refs = rest[:count]
    field_refs = rest[count : 2 * count]
    outs = rest[2 * count : 2 * count + groups]
    values, turned = rest[2 * count + groups :]
    tile_trials = sum(chunks)
    members = groups * tile_trials
    patches = mid_ref.shape[1] // LANES
    wide = patches + 2
    for d in range(groups):
        at = d * tile_trials
        for j, m in enumerate(chunks):
            ref = sample_refs[j * groups + d]
            for i in range(3):
                values[i, at : at + m, :] = ref[i]
            at += m
    meta = jnp.concatenate([left_ref[...], mid_ref[...], right_ref[...]], axis=1)
    deviation = [[None] * wide for _ in range(3)]
    gap = [[None] * wide for _ in range(3)]
    for i in range(3):
        for t in range(wide):
            cut = slice(t * LANES, (t + 1) * LANES)
            entry = values[i, :, cut].astype(f32)
            average = jnp.sum(entry, axis=0, keepdims=True) * (1.0 / members)
            deviation[i][t] = entry - average
            gap[i][t] = meta[8 * i : 8 * i + 1, cut] - average
    factor = float(members - 1)
    row_id = lax.broadcasted_iota(jnp.int32, (members, members), 0)
    col_id = lax.broadcasted_iota(jnp.int32, (members, members), 1)
    diagonal = row_id == col_id
    state = []
    for q in range(patches):
        pieces = []
        pull = jnp.zeros((members, LANES), f32)
        for i in range(3):
            for t in range(q, q + 3):
                cut = slice(t * LANES, (t + 1) * LANES)
                inverse = meta[8 * i + 1 : 8 * i + 2, cut]
                cell_y = meta[8 * i + 2 : 8 * i + 3, cut]
                cell_x = meta[8 * i + 3 : 8 * i + 4, cut]
                off_y = ((i - 1) * ROWS + cell_y - (ROWS - 1) / 2.0) / ROWS
                off_x = ((t - q - 1) * LANES + cell_x - (LANES - 1) / 2.0) / LANES
                local = inverse * jnp.exp(-0.5 * off_y * off_y - 0.5 * off_x * off_x)
                weight = jnp.sqrt(local * (1.0 / factor))
                pieces.append((deviation[i][t] * weight).astype(bf16))
                pull = pull + deviation[i][t] * (local * (1.0 / factor) * gap[i][t])
        scaled = jnp.concatenate(pieces, axis=1)
        gram = lax.dot_general(
            scaled, scaled, (((1,), (1,)), ((), ())), preferred_element_type=f32
        )
        system = jnp.where(diagonal, gram + 1.0, gram)
        squared = jnp.sum(system * system, axis=0, keepdims=True)
        squared = jnp.sum(squared, axis=1, keepdims=True)
        scale = jnp.sqrt(squared)
        state.append([system * (1.0 / scale), None, scale, jnp.sum(pull, axis=1, keepdims=True)])
    for step in range(NSIT):
        fine = step >= NSIT - 2
        for s in state:
            w, z = s[0], s[1]
            if fine:
                half = halves_of(w * -0.5)
                mul = lambda a: wide_product(halves_of(a), half)
            else:
                half = (w * -0.5).astype(bf16)
                mul = lambda a: product(a.astype(bf16), half)
            if z is None:
                s[1] = jnp.where(diagonal, 1.5, 0.0) - 0.5 * w
            else:
                s[1] = 1.5 * z + mul(z)
            if step < NSIT - 1:
                between = 1.5 * w + mul(w)
                s[0] = 1.5 * between + mul(between)
    for q in range(patches):
        _, z, scale, pull = state[q]
        root = z * lax.rsqrt(scale)
        once = jnp.sum(root * pull, axis=0, keepdims=True)
        gain = jnp.sum(root * once, axis=1, keepdims=True)
        middle = jnp.sum(root, axis=0, keepdims=True) * (1.0 / members)
        shift = gain - jnp.sum(gain, axis=0, keepdims=True) * (1.0 / members) + 1.0 / members
        mixing = ((root - middle) + shift).astype(bf16)
        pieces = []
        for y in range(ROWS):
            column = []
            for d in range(groups):
                for j in range(len(chunks)):
                    column.append(
                        field_refs[j * groups + d][y, :, q * LANES : (q + 1) * LANES]
                    )
            pieces.append(jnp.concatenate(column, axis=0))
        field = jnp.concatenate(pieces, axis=1)
        result = lax.dot_general(
            mixing, field, (((0,), (0,)), ((), ())), preferred_element_type=f32
        )
        for y in range(ROWS):
            turned[pl.ds(y, members, stride=ROWS), :] = result[:, y * LANES : (y + 1) * LANES]
        for d in range(groups):
            at = d * tile_trials * ROWS
            outs[d][:, :, q * LANES : (q + 1) * LANES] = (
                turned[at : at + tile_trials * ROWS, :]
                .reshape(tile_trials, ROWS, LANES)
                .astype(bf16)
            )


def transform(groups, chunks, meta, samples, fields):
    span = meta[1].shape[1]
    tile_trials = sum(chunks)
    members = groups * tile_trials
    args = tuple(meta) + tuple(samples) + tuple(fields)
    return call(
        functools.partial(transform_kernel, groups, chunks),
        [jax.ShapeDtypeStruct((tile_trials, ROWS, span), bf16) for _ in range(groups)],
        [
            pltpu.VMEM((3, members, span + 2 * LANES), bf16),
            pltpu.VMEM((members * ROWS, LANES), f32),
        ],
        4 * 10**9,
        4 * 2**20,
        args,
        [vmem()] * len(args),
    )


def gather_kernel(groups, me_ref, *rest):
    parts, out_ref = rest[:groups], rest[groups]
    span = parts[0].shape[2]
    me = me_ref[0]
    for d in range(groups):
        column = pl.multiple_of((me ^ d) * span, LANES)
        out_ref[:, :, pl.ds(column, span)] = parts[d][...]


def gathered(groups, me, parts):
    tile_trials, rows, span = parts[0].shape
    return call(
        functools.partial(gather_kernel, groups),
        [jax.ShapeDtypeStruct((tile_trials, rows, span * groups), bf16)],
        [],
        0,
        4 * tile_trials * rows * span * groups,
        (me,) + tuple(parts),
        [smem()] + [vmem()] * groups,
    )[0]


def across(parts):
    groups = len(parts)
    out = list(parts)
    for d in sorted(range(1, groups), reverse=True):
        out[d] = lax.ppermute(parts[d], "cols", [(i, i ^ d) for i in range(groups)])
    return out


def up_down(to_next, to_before, axis):
    count = lax.axis_size(axis)
    forward = [(i, i + 1) for i in range(count - 1)]
    back = [(j, i) for i, j in forward]
    return lax.ppermute(to_next, axis, forward), lax.ppermute(to_before, axis, back)


def on_device(
    prior_trials, courant, diffusion, obs_cell, obs_count, obs_value, error_kind, error_std
):
    tile_trials, _, width = prior_trials.shape
    groups = lax.axis_size("cols")
    own_count = obs_count.shape[1]
    slots = obs_cell.shape[2]
    me_scalar = lax.axis_index("cols").astype(jnp.int32)
    me = me_scalar[None]
    chunks = (tile_trials - BLOCK, BLOCK) if tile_trials > BLOCK else (tile_trials,)

    turned = jnp.transpose(prior_trials, (1, 0, 2))
    blank = jnp.zeros((BLOCK - 2 * FSTEPS, width), bf16)
    halos = []
    offset = 0
    for j, m in enumerate(chunks):
        pair = []
        for low in (ROWS - FSTEPS, 0):
            message = turned[low : low + FSTEPS, offset : offset + m].reshape(FSTEPS * m, width)
            if j == 0:
                message = jnp.concatenate(
                    [
                        message,
                        courant[low : low + FSTEPS],
                        diffusion[low : low + FSTEPS],
                        blank,
                    ],
                    axis=0,
                )
            pair.append(message)
        halos.append(up_down(pair[0], pair[1], "rows"))
        offset += m

    own_cell = lax.dynamic_slice_in_dim(obs_cell, me_scalar * own_count, own_count, 1)[0]
    live = jnp.arange(slots, dtype=jnp.int32)[None, :] < obs_count[0][:, None]
    table = 1.0 / (error_std * error_std)
    kinds = jnp.arange(error_std.shape[0], dtype=jnp.int32)
    looked = jnp.sum(jnp.where(error_kind[0][:, :, None] == kinds, table, 0.0), axis=-1)
    inverse = jnp.where(live, looked, 0.0)
    known = jnp.stack(
        [
            obs_value[0].reshape(-1),
            inverse.reshape(-1),
            (own_cell // LANES).astype(f32).reshape(-1),
            (own_cell % LANES).astype(f32).reshape(-1),
        ],
        axis=0,
    )
    known = jnp.pad(known, ((0, 4), (0, 0)))
    above, below = up_down(known, known, "rows")
    middle = jnp.concatenate([above, known, below], axis=0)
    left, right = up_down(middle[:, -LANES:], middle[:, :LANES], "cols")

    coef = None
    offset = 0
    samples, fields = [], []
    for j, m in enumerate(chunks):
        up, down = halos[j]
        extra = (courant, diffusion) if j == 0 else (coef,)
        made = forecast(j == 0, offset, m, groups, me, turned, up, down, extra, obs_cell[0])
        if j == 0:
            coef, made = made[0], made[1:]
        sampled, parts = made[0], made[1:]
        from_up, from_down = up_down(sampled, sampled, "rows")
        fields += across(parts)
        samples += across(spread_samples(groups, me, from_up, sampled, from_down))
        offset += m
    analysis = transform(groups, chunks, (left, middle, right), samples, fields)
    return gathered(groups, me, across(analysis))


def solution(mesh):
    placed = (
        P("cols", "rows", None),
        P("rows", None),
        P("rows", None),
        P("rows", None, None),
        P("rows", "cols"),
        P("rows", "cols", None),
        P("rows", "cols", None),
        P(),
    )
    return jax.shard_map(
        on_device, mesh=mesh, in_specs=placed, out_specs=P("cols", "rows", None), check_vma=False
    )
```

time: 159 us -> 114 us (0.72); the launches traced: 156 us -> 113 us
  waiting for transfers between devices: 58.8 us -> 31.3 us
  starting transfers between devices: 20.7 us -> 47.8 us
  Pallas kernels: 0 us -> 23.7 us
  matrix products: 17.9 us -> 0 us
  other arithmetic: 17 us -> 0.42 us
  blocking collectives: 16 us -> 0 us
  local copies, waits for them, and re-layouts: 24.9 us -> 9.03 us
    ppermute x6 -> x27, starting transfers between devices: 15.6 us -> 47.8 us  [the longest x6 23.1 us: up_down(): lax.ppermute(to_next, axis, forward)]
    pallas_call x0 -> x6, Pallas kernels: none -> 23.7 us  [call(): pl.pallas_call(kernel, out_shape=outs, in_specs=specs, out_specs=[vmem()...]
    dot_general x22 -> x0, matrix products: 17.9 us -> none  [the longest x6 3.89 us: transform(): inverse_root = jnp.dot(middle, inverse_root, precision=highest)]
    all_to_all x1 -> x0, blocking collectives: 16 us -> none  [on_device(): lax.all_to_all(analysis, 'cols', split_axis=0, concat_axis=2, tiled=True)]
    ppermute x6 -> x27, waiting for transfers between devices: 45.5 us -> 31.3 us  [the longest x15 24.9 us: across(): out[d] = lax.ppermute(parts[d], 'cols', [(i, i ^ d) for i in range(groups)])]
    all_to_all x1 -> x0, waiting for transfers between devices: 13.3 us -> none  [on_device(): lax.all_to_all(partition_sequence, 'cols', split_axis=2, concat_axis=0, t...]
    add x4 -> x0, other arithmetic: 8.74 us -> none  [the longest x3 8.74 us: one_step(): centre - speed_field * (centre - upwind)]
    unnamed x21 -> x73, local copies, waits for them, and re-layouts: 1.43 us -> 8.15 us
  transfers between devices with their start and end apart: 7 -> 27, of which waited for: 4 -> 11; matrix products, arithmetic and copies ran while one was open for 1% -> 1% of each run, Pallas kernels for 0% -> 13%
where the time goes in v1:
time: 114 us; the launch traced here: 113 us
  starting transfers between devices  47.8 us (42%)
  waiting for transfers between devices  31.3 us (27%)
  Pallas kernels  23.7 us (21%)
  local copies, waits for them, and re-layouts  9.03 us (8%)
    ppermute x15, waiting for transfers between devices, across(): out[d] = lax.ppermute(parts[d], 'cols', [(i, i ^ d) for i in range(groups)])  24.9 us
    pallas_call x6, Pallas kernels, call(): pl.pallas_call(kernel, out_shape=outs, in_specs=specs, out_specs=[vmem()...  23.7 us
    ppermute x6, starting transfers between devices, up_down(): lax.ppermute(to_next, axis, forward)  23.1 us
    ppermute x6, starting transfers between devices, up_down(): lax.ppermute(to_before, axis, back)  12.5 us
    ppermute x15, starting transfers between devices, across(): out[d] = lax.ppermute(parts[d], 'cols', [(i, i ^ d) for i in range(groups)])  12.3 us
    unnamed x73, local copies, waits for them, and re-layouts  8.15 us
    ppermute x6, waiting for transfers between devices, up_down(): lax.ppermute(to_before, axis, back)  3.52 us
    ppermute x6, waiting for transfers between devices, up_down(): lax.ppermute(to_next, axis, forward)  2.89 us
  transfers between devices with their start and end apart: 27, of which 11 were waited for; matrix products, arithmetic and copies ran while one was open for 1% of the time, Pallas kernels for 13%

profile of v1, /device:TPU:11, one launch (start us, length us, event | category | flops | bytes accessed | tf_op | source)
XLA Modules:
  0.0 112.7 jit_solution(11143134182127648883)
XLA Ops:
  3.0 3.2 %collective-permute-start.4 = (bf16[208,1024]{1,0:T(8,128)(2,1)S(1)}, bf16[208,1024]{1,0:T(8,128)(2,1)S(1)}, u32[]{:S(2)}, u32[]{:S(2)}) collective-permute-start(bf16[208,1024]{1,0:T(8,128)(2,1)S(1)} %get-tuple-element.64), channel_id=1, source_target_pairs={{0,1},{1,2},{2,3},{3,4},{4,5},{5,6},{6,7},{8,9},{9,10},{10,11},{11... | collective-permute-start | bytes 1277960 | tf_op jit(solution)/shard_map/ppermute | solution.py:358
  6.1 2.1 %collective-permute-start.5 = (bf16[208,1024]{1,0:T(8,128)(2,1)S(1)}, bf16[208,1024]{1,0:T(8,128)(2,1)S(1)}, u32[]{:S(2)}, u32[]{:S(2)}) collective-permute-start(bf16[208,1024]{1,0:T(8,128)(2,1)S(1)} %get-tuple-element.63), channel_id=1, source_target_pairs={{1,0},{2,1},{3,2},{4,3},{5,4},{6,5},{7,6},{9,8},{10,9},{11,10},{12... | collective-permute-start | bytes 1277960 | tf_op jit(solution)/shard_map/ppermute | solution.py:358
  11.8 4.1 %collective-permute-start = (f32[8,256]{1,0:T(8,128)S(1)}, f32[8,256]{1,0:T(8,128)S(1)}, u32[]{:S(2)}, u32[]{:S(2)}) collective-permute-start(f32[8,256]{1,0:T(8,128)S(1)} %select_maximum_fusion), channel_id=1, source_target_pairs={{0,1},{1,2},{2,3},{3,4},{4,5},{5,6},{6,7},{8,9},{9,10},{10,11},{11... | collective-permute-start | bytes 24584 | tf_op jit(solution)/shard_map/ppermute | solution.py:358
  15.9 1.9 %collective-permute-start.1 = (f32[8,256]{1,0:T(8,128)S(1)}, f32[8,256]{1,0:T(8,128)S(1)}, u32[]{:S(2)}, u32[]{:S(2)}) collective-permute-start(f32[8,256]{1,0:T(8,128)S(1)} %select_maximum_fusion), channel_id=1, source_target_pairs={{1,0},{2,1},{3,2},{4,3},{5,4},{6,5},{7,6},{9,8},{10,9},{11,10},{12... | collective-permute-start | bytes 24584 | tf_op jit(solution)/shard_map/ppermute | solution.py:358
  17.9 4.3 %collective-permute-start.11 = (bf16[64,1024]{1,0:T(8,128)(2,1)S(1)}, bf16[64,1024]{1,0:T(8,128)(2,1)S(1)}, u32[]{:S(2)}, u32[]{:S(2)}) collective-permute-start(bf16[64,1024]{1,0:T(8,128)(2,1)S(1)} %bitcast.21), channel_id=1, source_target_pairs={{0,1},{1,2},{2,3},{3,4},{4,5},{5,6},{6,7},{8,9},{9,10},{10,11},{11... | collective-permute-start | bytes 393224 | tf_op jit(solution)/shard_map/ppermute | solution.py:358
  22.1 2.9 %collective-permute-done = f32[8,256]{1,0:T(8,128)S(1)} collective-permute-done((f32[8,256]{1,0:T(8,128)S(1)}, f32[8,256]{1,0:T(8,128)S(1)}, u32[]{:S(2)}, u32[]{:S(2)}) %collective-permute-start) | collective-permute-done | bytes 8224 | tf_op jit(solution)/shard_map/ppermute | solution.py:358
  25.0 1.9 %collective-permute-start.12 = (bf16[64,1024]{1,0:T(8,128)(2,1)S(1)}, bf16[64,1024]{1,0:T(8,128)(2,1)S(1)}, u32[]{:S(2)}, u32[]{:S(2)}) collective-permute-start(bf16[64,1024]{1,0:T(8,128)(2,1)S(1)} %bitcast.20), channel_id=1, source_target_pairs={{1,0},{2,1},{3,2},{4,3},{5,4},{6,5},{7,6},{9,8},{10,9},{11,10},{12... | collective-permute-start | bytes 393224 | tf_op jit(solution)/shard_map/ppermute | solution.py:358
  28.8 7.3 %shard_map.82 = (f32[3,16,1024]{2,1,0:T(8,128)}, bf16[48,1024]{1,0:T(8,128)(2,1)}, bf16[8,48,256]{2,1,0:T(8,128)(2,1)}, bf16[8,48,256]{2,1,0:T(8,128)(2,1)}, bf1...) custom-call(s32[1]{0:T(128)} %bitcast.me_ref, bf16[8,64,1024]{2,1,0:T(8,128)(2,1)} %bitcast.16, ...), custom_call_target="tpu_custom_call" | custom-call | flops 34603008 | bytes 2949120 | tf_op jit(solution)/shard_map/pallas_call | solution.py:23
  37.9 3.0 %collective-permute-start.2 = (f32[24,128]{1,0:T(8,128)S(1)}, f32[24,128]{1,0:T(8,128)S(1)}, u32[]{:S(2)}, u32[]{:S(2)}) collective-permute-start(f32[24,128]{1,0:T(8,128)S(1)} %get-tuple-element.58), channel_id=1, source_target_pairs={{0,8},{8,16},{16,24},{1,9},{9,17},{17,25},{2,10},{10,18},{18,26},{... | collective-permute-start | bytes 36872 | tf_op jit(solution)/shard_map/ppermute | solution.py:358
  41.7 3.9 %shard_map.84 = (bf16[16,1024]{1,0:T(8,128)(2,1)}, bf16[8,16,256]{2,1,0:T(8,128)(2,1)}, bf16[8,16,256]{2,1,0:T(8,128)(2,1)}, bf16[8,16,256]{2,1,0:T(8,128)(2,1)}, bf16[8,16,256]{2,1,0:T(8,128)(2,1)}) custom-call(s32[1]{0:T(128)} %bitcast.me_ref, bf16[8,64,1024]{2,1,0:T(8,128)(2,1)} %bitcast.17, bf16[64,1024]{1,0:T(8,128)(2,1)} %copy-done.6, ...), custom_call_target="tpu_custom_call" | custom-call | flops 11534336 | bytes 983040 | tf_op jit(solution)/shard_map/pallas_call | solution.py:23
  45.6 4.5 %collective-permute-start.13 = (bf16[16,1024]{1,0:T(8,128)(2,1)}, bf16[16,1024]{1,0:T(8,128)(2,1)S(1)}, u32[]{:S(2)}, u32[]{:S(2)}) collective-permute-start(bf16[16,1024]{1,0:T(8,128)(2,1)} %get-tuple-element.34.own_ref), channel_id=1, source_target_pairs={{0,1},{1,2},{2,3},{3,4},{4,5},{5,6},{6,7},{8,9},{9,10},{10,11},{11... | collective-permute-start | bytes 98312 | tf_op jit(solution)/shard_map/ppermute | solution.py:358
  50.2 1.9 %collective-permute-start.14 = (bf16[16,1024]{1,0:T(8,128)(2,1)}, bf16[16,1024]{1,0:T(8,128)(2,1)S(1)}, u32[]{:S(2)}, u32[]{:S(2)}) collective-permute-start(bf16[16,1024]{1,0:T(8,128)(2,1)} %get-tuple-element.34.own_ref), channel_id=1, source_target_pairs={{1,0},{2,1},{3,2},{4,3},{5,4},{6,5},{7,6},{9,8},{10,9},{11,10},{12... | collective-permute-start | bytes 98312 | tf_op jit(solution)/shard_map/ppermute | solution.py:358
  52.1 2.7 %collective-permute-start.3 = (f32[24,128]{1,0:T(8,128)S(1)}, f32[24,128]{1,0:T(8,128)S(1)}, u32[]{:S(2)}, u32[]{:S(2)}) collective-permute-start(f32[24,128]{1,0:T(8,128)S(1)} %get-tuple-element.57), channel_id=1, source_target_pairs={{8,0},{16,8},{24,16},{9,1},{17,9},{25,17},{10,2},{18,10},{26,18},{... | collective-permute-start | bytes 36872 | tf_op jit(solution)/shard_map/ppermute | solution.py:358
  54.8 2.6 %collective-permute-done.3.right_ref = f32[24,128]{1,0:T(8,128)S(1)} collective-permute-done((f32[24,128]{1,0:T(8,128)S(1)}, f32[24,128]{1,0:T(8,128)S(1)}, u32[]{:S(2)}, u32[]{:S(2)}) %collective-permute-start.3) | collective-permute-done | bytes 12320 | tf_op jit(solution)/shard_map/ppermute | solution.py:358
  57.4 4.0 %collective-permute-start.6 = (bf16[48,1024]{1,0:T(8,128)(2,1)S(1)}, bf16[48,1024]{1,0:T(8,128)(2,1)S(1)}, u32[]{:S(2)}, u32[]{:S(2)}) collective-permute-start(bf16[48,1024]{1,0:T(8,128)(2,1)S(1)} %copy-done.9), channel_id=1, source_target_pairs={{0,1},{1,2},{2,3},{3,4},{4,5},{5,6},{6,7},{8,9},{9,10},{10,11},{11... | collective-permute-start | bytes 294920 | tf_op jit(solution)/shard_map/ppermute | solution.py:358
  61.4 1.9 %collective-permute-start.7 = (bf16[48,1024]{1,0:T(8,128)(2,1)S(1)}, bf16[48,1024]{1,0:T(8,128)(2,1)S(1)}, u32[]{:S(2)}, u32[]{:S(2)}) collective-permute-start(bf16[48,1024]{1,0:T(8,128)(2,1)S(1)} %copy-done.9), channel_id=1, source_target_pairs={{1,0},{2,1},{3,2},{4,3},{5,4},{6,5},{7,6},{9,8},{10,9},{11,10},{12... | collective-permute-start | bytes 294920 | tf_op jit(solution)/shard_map/ppermute | solution.py:358
  71.6 1.8 %shard_map.83 = (bf16[3,48,512]{2,1,0:T(8,128)(2,1)}, bf16[3,48,512]{2,1,0:T(8,128)(2,1)}, bf16[3,48,512]{2,1,0:T(8,128)(2,1)}, bf16[3,48,512]{2,1,0:T(8,128)(2,1)}) custom-call(s32[1]{0:T(128)} %bitcast.me_ref, bf16[48,1024]{1,0:T(8,128)(2,1)} %copy-done.10, bf16[48,1024]{1,0:T(8,128)(2,1)} %get-tuple-element.28.own_ref, bf16[48,1024]{1,0:T(8,128)(2,1)} %copy-done.11), custom_call_target="tpu_custom_call" | custom-call | bytes 589824 | tf_op jit(solution)/shard_map/pallas_call | solution.py:23
  73.5 2.0 %collective-permute-done.16.rest_6_ = bf16[3,16,512]{2,1,0:T(8,128)(2,1)S(1)} collective-permute-done((bf16[3,16,512]{2,1,0:T(8,128)(2,1)}, bf16[3,16,512]{2,1,0:T(8,128)(2,1)S(1)}, u32[]{:S(2)}, u32[]{:S(2)}) %collective-permute-start.16) | collective-permute-done | bytes 49184 | tf_op jit(solution)/shard_map/ppermute | solution.py:350
  79.0 3.4 %collective-permute-done.20.rest_11_ = bf16[8,48,256]{2,1,0:T(8,128)(2,1)S(1)} collective-permute-done((bf16[8,48,256]{2,1,0:T(8,128)(2,1)S(1)}, bf16[8,48,256]{2,1,0:T(8,128)(2,1)S(1)}, u32[]{:S(2)}, u32[]{:S(2)}) %collective-permute-start.20) | collective-permute-done | bytes 196640 | tf_op jit(solution)/shard_map/ppermute | solution.py:350
  82.4 2.9 %collective-permute-done.10.rest_3_ = bf16[3,48,512]{2,1,0:T(8,128)(2,1)S(1)} collective-permute-done((bf16[3,48,512]{2,1,0:T(8,128)(2,1)}, bf16[3,48,512]{2,1,0:T(8,128)(2,1)S(1)}, u32[]{:S(2)}, u32[]{:S(2)}) %collective-permute-start.10) | collective-permute-done | bytes 147488 | tf_op jit(solution)/shard_map/ppermute | solution.py:350
  87.7 6.9 %shard_map.86 = (bf16[64,8,256]{2,1,0:T(8,128)(2,1)}, bf16[64,8,256]{2,1,0:T(8,128)(2,1)}, bf16[64,8,256]{2,1,0:T(8,128)(2,1)}, bf16[64,8,256]{2,1,0:T(8,128)(2,1)}) custom-call(f32[24,128]{1,0:T(8,128)} %copy-done.33, f32[24,256]{1,0:T(8,128)} %copy-done.8, f32[24,128]{1,0:T(8,128)} %copy-done.34, bf16[3,48,512]{2,1,0:T(8,128)(2,1)} %get-tuple-element.29.rest_0_, ...), custom_call_target="tpu_custom_call" | custom-call | flops 4000000000 | bytes 4194304 | tf_op jit(solution)/shard_map/pallas_call | solution.py:23
  97.6 6.4 %collective-permute-done.25.rest_2_ = bf16[64,8,256]{2,1,0:T(8,128)(2,1)S(1)} collective-permute-done((bf16[64,8,256]{2,1,0:T(8,128)(2,1)}, bf16[64,8,256]{2,1,0:T(8,128)(2,1)S(1)}, u32[]{:S(2)}, u32[]{:S(2)}) %collective-permute-start.25) | collective-permute-done | bytes 262176 | tf_op jit(solution)/shard_map/ppermute | solution.py:350
  104.0 5.8 %collective-permute-done.26.rest_3_ = bf16[64,8,256]{2,1,0:T(8,128)(2,1)S(1)} collective-permute-done((bf16[64,8,256]{2,1,0:T(8,128)(2,1)}, bf16[64,8,256]{2,1,0:T(8,128)(2,1)S(1)}, u32[]{:S(2)}, u32[]{:S(2)}) %collective-permute-start.26) | collective-permute-done | bytes 262176 | tf_op jit(solution)/shard_map/ppermute | solution.py:350
  110.4 2.3 %shard_map.87 = bf16[64,8,1024]{2,1,0:T(8,128)(2,1)} custom-call(s32[1]{0:T(128)} %bitcast.me_ref, bf16[64,8,256]{2,1,0:T(8,128)(2,1)} %get-tuple-element.47.rest_0_, bf16[64,8,256]{2,1,0:T(8,128)(2,1)} %copy-done.3, bf16[64,8,256]{2,1,0:T(8,128)(2,1)} %copy-done.4, bf16[64,8,256]{2,1,0:T(8,128)(2,1)} %copy-done.5), custom_call_target="tpu_custom_call" | custom-call | bytes 2097152 | tf_op jit(solution)/shard_map/pallas_call | solution.py:23
  (124 shorter events, 28.6 us)
Async XLA Ops:
  3.0 24.9 %collective-permute-start.4 = (bf16[208,1024]{1,0:T(8,128)(2,1)S(1)}, bf16[208,1024]{1,0:T(8,128)(2,1)S(1)}, u32[]{:S(2)}, u32[]{:S(2)}) collective-permute-start(bf16[208,1024]{1,0:T(8,128)(2,1)S(1)} %get-tuple-element.64), channel_id=1, source_target_pairs={{0,1},{1,2},{2,3},{3,4},{4,5},{5,6},{6,7},{8,9},{9,10},{10,11},{11... | collective-permute-start | bytes 1277960 | tf_op jit(solution)/shard_map/ppermute | solution.py:358
  6.1 21.7 %collective-permute-start.5 = (bf16[208,1024]{1,0:T(8,128)(2,1)S(1)}, bf16[208,1024]{1,0:T(8,128)(2,1)S(1)}, u32[]{:S(2)}, u32[]{:S(2)}) collective-permute-start(bf16[208,1024]{1,0:T(8,128)(2,1)S(1)} %get-tuple-element.63), channel_id=1, source_target_pairs={{1,0},{2,1},{3,2},{4,3},{5,4},{6,5},{7,6},{9,8},{10,9},{11,10},{12... | collective-permute-start | bytes 1277960 | tf_op jit(solution)/shard_map/ppermute | solution.py:358
  11.8 13.2 %collective-permute-start = (f32[8,256]{1,0:T(8,128)S(1)}, f32[8,256]{1,0:T(8,128)S(1)}, u32[]{:S(2)}, u32[]{:S(2)}) collective-permute-start(f32[8,256]{1,0:T(8,128)S(1)} %select_maximum_fusion), channel_id=1, source_target_pairs={{0,1},{1,2},{2,3},{3,4},{4,5},{5,6},{6,7},{8,9},{9,10},{10,11},{11... | collective-permute-start | bytes 24584 | tf_op jit(solution)/shard_map/ppermute | solution.py:358
  15.9 11.9 %collective-permute-start.1 = (f32[8,256]{1,0:T(8,128)S(1)}, f32[8,256]{1,0:T(8,128)S(1)}, u32[]{:S(2)}, u32[]{:S(2)}) collective-permute-start(f32[8,256]{1,0:T(8,128)S(1)} %select_maximum_fusion), channel_id=1, source_target_pairs={{1,0},{2,1},{3,2},{4,3},{5,4},{6,5},{7,6},{9,8},{10,9},{11,10},{12... | collective-permute-start | bytes 24584 | tf_op jit(solution)/shard_map/ppermute | solution.py:358
  17.9 23.1 %collective-permute-start.11 = (bf16[64,1024]{1,0:T(8,128)(2,1)S(1)}, bf16[64,1024]{1,0:T(8,128)(2,1)S(1)}, u32[]{:S(2)}, u32[]{:S(2)}) collective-permute-start(bf16[64,1024]{1,0:T(8,128)(2,1)S(1)} %bitcast.21), channel_id=1, source_target_pairs={{0,1},{1,2},{2,3},{3,4},{4,5},{5,6},{6,7},{8,9},{9,10},{10,11},{11... | collective-permute-start | bytes 393224 | tf_op jit(solution)/shard_map/ppermute | solution.py:358
  25.0 16.0 %collective-permute-start.12 = (bf16[64,1024]{1,0:T(8,128)(2,1)S(1)}, bf16[64,1024]{1,0:T(8,128)(2,1)S(1)}, u32[]{:S(2)}, u32[]{:S(2)}) collective-permute-start(bf16[64,1024]{1,0:T(8,128)(2,1)S(1)} %bitcast.20), channel_id=1, source_target_pairs={{1,0},{2,1},{3,2},{4,3},{5,4},{6,5},{7,6},{9,8},{10,9},{11,10},{12... | collective-permute-start | bytes 393224 | tf_op jit(solution)/shard_map/ppermute | solution.py:358
  36.1 42.1 %collective-permute-start.18 = (bf16[8,48,256]{2,1,0:T(8,128)(2,1)}, bf16[8,48,256]{2,1,0:T(8,128)(2,1)S(1)}, u32[]{:S(2)}, u32[]{:S(2)}) collective-permute-start(bf16[8,48,256]{2,1,0:T(8,128)(2,1)} %get-tuple-element.40), channel_id=1, source_target_pairs={{0,8},{8,0},{16,24},{24,16},{1,9},{9,1},{17,25},{25,17},{2,10},{10... | collective-permute-start | bytes 589832 | tf_op jit(solution)/shard_map/ppermute | solution.py:350
  37.9 14.2 %collective-permute-start.2 = (f32[24,128]{1,0:T(8,128)S(1)}, f32[24,128]{1,0:T(8,128)S(1)}, u32[]{:S(2)}, u32[]{:S(2)}) collective-permute-start(f32[24,128]{1,0:T(8,128)S(1)} %get-tuple-element.58), channel_id=1, source_target_pairs={{0,8},{8,16},{16,24},{1,9},{9,17},{17,25},{2,10},{10,18},{18,26},{... | collective-permute-start | bytes 36872 | tf_op jit(solution)/shard_map/ppermute | solution.py:358
  45.6 17.8 %collective-permute-start.21 = (bf16[8,16,256]{2,1,0:T(8,128)(2,1)}, bf16[8,16,256]{2,1,0:T(8,128)(2,1)S(1)}, u32[]{:S(2)}, u32[]{:S(2)}) collective-permute-start(bf16[8,16,256]{2,1,0:T(8,128)(2,1)} %get-tuple-element.44), channel_id=1, source_target_pairs={{0,8},{8,0},{16,24},{24,16},{1,9},{9,1},{17,25},{25,17},{2,10},{10... | collective-permute-start | bytes 196616 | tf_op jit(solution)/shard_map/ppermute | solution.py:350
  45.6 11.8 %collective-permute-start.13 = (bf16[16,1024]{1,0:T(8,128)(2,1)}, bf16[16,1024]{1,0:T(8,128)(2,1)S(1)}, u32[]{:S(2)}, u32[]{:S(2)}) collective-permute-start(bf16[16,1024]{1,0:T(8,128)(2,1)} %get-tuple-element.34.own_ref), channel_id=1, source_target_pairs={{0,1},{1,2},{2,3},{3,4},{4,5},{5,6},{6,7},{8,9},{9,10},{10,11},{11... | collective-permute-start | bytes 98312 | tf_op jit(solution)/shard_map/ppermute | solution.py:358
  50.2 11.3 %collective-permute-start.14 = (bf16[16,1024]{1,0:T(8,128)(2,1)}, bf16[16,1024]{1,0:T(8,128)(2,1)S(1)}, u32[]{:S(2)}, u32[]{:S(2)}) collective-permute-start(bf16[16,1024]{1,0:T(8,128)(2,1)} %get-tuple-element.34.own_ref), channel_id=1, source_target_pairs={{1,0},{2,1},{3,2},{4,3},{5,4},{6,5},{7,6},{9,8},{10,9},{11,10},{12... | collective-permute-start | bytes 98312 | tf_op jit(solution)/shard_map/ppermute | solution.py:358
  52.1 5.3 %collective-permute-start.3 = (f32[24,128]{1,0:T(8,128)S(1)}, f32[24,128]{1,0:T(8,128)S(1)}, u32[]{:S(2)}, u32[]{:S(2)}) collective-permute-start(f32[24,128]{1,0:T(8,128)S(1)} %get-tuple-element.57), channel_id=1, source_target_pairs={{8,0},{16,8},{24,16},{9,1},{17,9},{25,17},{10,2},{18,10},{26,18},{... | collective-permute-start | bytes 36872 | tf_op jit(solution)/shard_map/ppermute | solution.py:358
  57.4 8.5 %collective-permute-start.22 = (bf16[8,16,256]{2,1,0:T(8,128)(2,1)}, bf16[8,16,256]{2,1,0:T(8,128)(2,1)S(1)}, u32[]{:S(2)}, u32[]{:S(2)}) collective-permute-start(bf16[8,16,256]{2,1,0:T(8,128)(2,1)} %get-tuple-element.45), channel_id=1, source_target_pairs={{0,16},{8,24},{16,0},{24,8},{1,17},{9,25},{17,1},{25,9},{2,18},{10... | collective-permute-start | bytes 196616 | tf_op jit(solution)/shard_map/ppermute | solution.py:350
  57.4 12.4 %collective-permute-start.6 = (bf16[48,1024]{1,0:T(8,128)(2,1)S(1)}, bf16[48,1024]{1,0:T(8,128)(2,1)S(1)}, u32[]{:S(2)}, u32[]{:S(2)}) collective-permute-start(bf16[48,1024]{1,0:T(8,128)(2,1)S(1)} %copy-done.9), channel_id=1, source_target_pairs={{0,1},{1,2},{2,3},{3,4},{4,5},{5,6},{6,7},{8,9},{9,10},{10,11},{11... | collective-permute-start | bytes 294920 | tf_op jit(solution)/shard_map/ppermute | solution.py:358
  61.4 9.0 %collective-permute-start.7 = (bf16[48,1024]{1,0:T(8,128)(2,1)S(1)}, bf16[48,1024]{1,0:T(8,128)(2,1)S(1)}, u32[]{:S(2)}, u32[]{:S(2)}) collective-permute-start(bf16[48,1024]{1,0:T(8,128)(2,1)S(1)} %copy-done.9), channel_id=1, source_target_pairs={{1,0},{2,1},{3,2},{4,3},{5,4},{6,5},{7,6},{9,8},{10,9},{11,10},{12... | collective-permute-start | bytes 294920 | tf_op jit(solution)/shard_map/ppermute | solution.py:358
  68.3 10.6 %collective-permute-start.19 = (bf16[8,48,256]{2,1,0:T(8,128)(2,1)S(1)}, bf16[8,48,256]{2,1,0:T(8,128)(2,1)S(1)}, u32[]{:S(2)}, u32[]{:S(2)}) collective-permute-start(bf16[8,48,256]{2,1,0:T(8,128)(2,1)S(1)} %copy-done.21), channel_id=1, source_target_pairs={{0,16},{8,24},{16,0},{24,8},{1,17},{9,25},{17,1},{25,9},{2,18},{10... | collective-permute-start | bytes 589832 | tf_op jit(solution)/shard_map/ppermute | solution.py:350
  69.1 6.4 %collective-permute-start.16 = (bf16[3,16,512]{2,1,0:T(8,128)(2,1)}, bf16[3,16,512]{2,1,0:T(8,128)(2,1)S(1)}, u32[]{:S(2)}, u32[]{:S(2)}) collective-permute-start(bf16[3,16,512]{2,1,0:T(8,128)(2,1)} %get-tuple-element.37), channel_id=1, source_target_pairs={{0,16},{8,24},{16,0},{24,8},{1,17},{9,25},{17,1},{25,9},{2,18},{10... | collective-permute-start | bytes 147464 | tf_op jit(solution)/shard_map/ppermute | solution.py:350
  69.8 8.4 %collective-permute-start.17 = (bf16[3,16,512]{2,1,0:T(8,128)(2,1)}, bf16[3,16,512]{2,1,0:T(8,128)(2,1)S(1)}, u32[]{:S(2)}, u32[]{:S(2)}) collective-permute-start(bf16[3,16,512]{2,1,0:T(8,128)(2,1)} %get-tuple-element.38), channel_id=1, source_target_pairs={{0,24},{8,16},{16,8},{24,0},{1,25},{9,17},{17,9},{25,1},{2,26},{10... | collective-permute-start | bytes 147464 | tf_op jit(solution)/shard_map/ppermute | solution.py:350
  70.5 11.9 %collective-permute-start.20 = (bf16[8,48,256]{2,1,0:T(8,128)(2,1)S(1)}, bf16[8,48,256]{2,1,0:T(8,128)(2,1)S(1)}, u32[]{:S(2)}, u32[]{:S(2)}) collective-permute-start(bf16[8,48,256]{2,1,0:T(8,128)(2,1)S(1)} %copy-done.20), channel_id=1, source_target_pairs={{0,24},{8,16},{16,8},{24,0},{1,25},{9,17},{17,9},{25,1},{2,26},{10... | collective-permute-start | bytes 589832 | tf_op jit(solution)/shard_map/ppermute | solution.py:350
  75.5 9.8 %collective-permute-start.10 = (bf16[3,48,512]{2,1,0:T(8,128)(2,1)}, bf16[3,48,512]{2,1,0:T(8,128)(2,1)S(1)}, u32[]{:S(2)}, u32[]{:S(2)}) collective-permute-start(bf16[3,48,512]{2,1,0:T(8,128)(2,1)} %get-tuple-element.32), channel_id=1, source_target_pairs={{0,24},{8,16},{16,8},{24,0},{1,25},{9,17},{17,9},{25,1},{2,26},{10... | collective-permute-start | bytes 442376 | tf_op jit(solution)/shard_map/ppermute | solution.py:350
  78.2 7.1 %collective-permute-start.8 = (bf16[3,48,512]{2,1,0:T(8,128)(2,1)}, bf16[3,48,512]{2,1,0:T(8,128)(2,1)S(1)}, u32[]{:S(2)}, u32[]{:S(2)}) collective-permute-start(bf16[3,48,512]{2,1,0:T(8,128)(2,1)} %get-tuple-element.30), channel_id=1, source_target_pairs={{0,8},{8,0},{16,24},{24,16},{1,9},{9,1},{17,25},{25,17},{2,10},{10... | collective-permute-start | bytes 442376 | tf_op jit(solution)/shard_map/ppermute | solution.py:350
  78.2 8.9 %collective-permute-start.9 = (bf16[3,48,512]{2,1,0:T(8,128)(2,1)}, bf16[3,48,512]{2,1,0:T(8,128)(2,1)S(1)}, u32[]{:S(2)}, u32[]{:S(2)}) collective-permute-start(bf16[3,48,512]{2,1,0:T(8,128)(2,1)} %get-tuple-element.31), channel_id=1, source_target_pairs={{0,16},{8,24},{16,0},{24,8},{1,17},{9,25},{17,1},{25,9},{2,18},{10... | collective-permute-start | bytes 442376 | tf_op jit(solution)/shard_map/ppermute | solution.py:350
  95.9 8.1 %collective-permute-start.25 = (bf16[64,8,256]{2,1,0:T(8,128)(2,1)}, bf16[64,8,256]{2,1,0:T(8,128)(2,1)S(1)}, u32[]{:S(2)}, u32[]{:S(2)}) collective-permute-start(bf16[64,8,256]{2,1,0:T(8,128)(2,1)} %get-tuple-element.49), channel_id=1, source_target_pairs={{0,16},{8,24},{16,0},{24,8},{1,17},{9,25},{17,1},{25,9},{2,18},{10... | collective-permute-start | bytes 786440 | tf_op jit(solution)/shard_map/ppermute | solution.py:350
  96.4 13.4 %collective-permute-start.26 = (bf16[64,8,256]{2,1,0:T(8,128)(2,1)}, bf16[64,8,256]{2,1,0:T(8,128)(2,1)S(1)}, u32[]{:S(2)}, u32[]{:S(2)}) collective-permute-start(bf16[64,8,256]{2,1,0:T(8,128)(2,1)} %get-tuple-element.50), channel_id=1, source_target_pairs={{0,24},{8,16},{16,8},{24,0},{1,25},{9,17},{17,9},{25,1},{2,26},{10... | collective-permute-start | bytes 786440 | tf_op jit(solution)/shard_map/ppermute | solution.py:350
  (39 other events, 270.8 us)

commit v2 on v1

v2 whole, which is shorter than its diff:
```python
import functools
import math
import jax
import jax.numpy as jnp
from jax import lax
from jax.experimental import pallas as pl
from jax.experimental.pallas import tpu as pltpu
from jax.sharding import PartitionSpec as P

ROWS = 8
LANES = 128
FSTEPS = 4
NSIT = 6
BLOCK = 16
SLACK = 12 * 1024 * 1024
f32 = jnp.float32
bf16 = jnp.bfloat16

vmem = functools.partial(pl.BlockSpec, memory_space=pltpu.VMEM)
smem = functools.partial(pl.BlockSpec, memory_space=pltpu.SMEM)


def call(kernel, outs, scratch, flops, args, specs):
    moved = sum(x.size * x.dtype.itemsize for x in tuple(args) + tuple(outs))
    held = sum(math.prod(x.shape) * jnp.dtype(x.dtype).itemsize for x in scratch)
    return pl.pallas_call(
        kernel,
        out_shape=outs,
        in_specs=specs,
        out_specs=[vmem() for _ in outs],
        scratch_shapes=scratch,
        compiler_params=pltpu.CompilerParams(vmem_limit_bytes=moved + held + SLACK),
        cost_estimate=pl.CostEstimate(flops=flops, bytes_accessed=moved, transcendentals=0),
    )(*args)


def pack_kernel(chunks, place_ref, prior_ref, speed_ref, spread_ref, *rest):
    messages, flat = rest[:-1], rest[-1]
    odd = place_ref[1]

    def fill(first_low, second_low):
        offset = 0
        for j, m in enumerate(chunks):
            pair = messages[2 * j : 2 * j + 2]

            def block(i, carry):
                start = pl.multiple_of(i * BLOCK, BLOCK)
                for t in range(flat.shape[0]):
                    cut = slice(t * LANES, (t + 1) * LANES)
                    entry = prior_ref[pl.ds(offset + start, BLOCK), :, cut].astype(f32)
                    flat[t] = entry.reshape(BLOCK * ROWS, LANES)
                    for ref, low in zip(pair, (first_low, second_low)):
                        for r in range(FSTEPS):
                            at = pl.multiple_of(r * m + start, BLOCK)
                            ref[pl.ds(at, BLOCK), cut] = flat[
                                t, pl.ds(low + r, BLOCK, stride=ROWS), :
                            ].astype(bf16)
                return carry

            lax.fori_loop(0, m // BLOCK, block, 0)
            if j == 0:
                speed = speed_ref[...].astype(f32)
                spread = spread_ref[...].astype(f32)
                blank = jnp.zeros((BLOCK - 2 * FSTEPS, speed.shape[1]), f32)
                for ref, low in zip(pair, (first_low, second_low)):
                    ref[FSTEPS * m :, :] = jnp.concatenate(
                        [speed[low : low + FSTEPS], spread[low : low + FSTEPS], blank], axis=0
                    ).astype(bf16)
            offset += m

    pl.when(odd == 1)(lambda: fill(0, FSTEPS))
    pl.when(odd == 0)(lambda: fill(FSTEPS, 0))


def packed(chunks, place, prior, speed, spread):
    width = prior.shape[2]
    outs = []
    for j, m in enumerate(chunks):
        rows = FSTEPS * m + (BLOCK if j == 0 else 0)
        outs += [jax.ShapeDtypeStruct((rows, width), bf16)] * 2
    return call(
        functools.partial(pack_kernel, chunks),
        outs,
        [pltpu.VMEM((width // LANES, BLOCK * ROWS, LANES), f32)],
        0,
        (place, prior, speed, spread),
        [smem()] + [vmem()] * 3,
    )


def thirds_of(x):
    high = x.astype(bf16).astype(f32)
    middle = (x - high).astype(bf16).astype(f32)
    return [high, middle, (x - high) - middle]


def describe(m, me, sample_ref, cell_ref, value_ref, kind_ref, count_ref, std_ref):
    sample_ref[m : m + BLOCK, :] = jnp.zeros((BLOCK, sample_ref.shape[1]), bf16)
    own_count, slots = value_ref.shape[1:]
    slot = lax.broadcasted_iota(jnp.int32, (1, slots), 1)
    blank = jnp.zeros((BLOCK - 8, slots), f32)
    for q in range(own_count):
        patch = me * own_count + q
        cell = cell_ref[pl.ds(patch, 1), :]
        kind = kind_ref[0, q : q + 1, :]
        inverse = jnp.zeros((1, slots), f32)
        for k in range(std_ref.shape[0]):
            deviation = jnp.full((1, slots), std_ref[k], f32)
            inverse = jnp.where(kind == k, 1.0 / (deviation * deviation), inverse)
        inverse = jnp.where(slot < count_ref[0, q], inverse, 0.0)
        terms = thirds_of(value_ref[0, q : q + 1, :]) + thirds_of(inverse)
        terms += [(cell // LANES).astype(f32), (cell % LANES).astype(f32), blank]
        column = pl.multiple_of(patch * LANES, LANES)
        sample_ref[m : m + BLOCK, pl.ds(column, LANES)] = jnp.concatenate(
            terms, axis=0
        ).astype(bf16)


def forecast_kernel(
    first, m, place_ref, near_ref, far_ref, from_near_ref, from_far_ref, cell_ref, *rest
):
    if first:
        value_ref, kind_ref, count_ref, std_ref, coef_ref, sample_ref = rest[:6]
        rest = rest[6:]
        before = 0
    else:
        coef_ref, earlier_ref, sample_ref = rest[:3]
        rest = rest[3:]
        before = earlier_ref.shape[0] - BLOCK
        sample_ref[:before, :] = earlier_ref[:before, :]
        sample_ref[before + m :, :] = earlier_ref[before:, :]
    field_ref, even, odd = rest
    width = near_ref.shape[1]
    tiles = width // LANES
    total = ROWS + 2 * FSTEPS
    me, is_odd = place_ref[0], place_ref[1]
    sources = (
        (from_near_ref, (1 - is_odd) * (FSTEPS + ROWS)),
        (near_ref, FSTEPS + (1 - is_odd) * FSTEPS),
        (far_ref, FSTEPS + is_odd * FSTEPS),
        (from_far_ref, is_odd * (FSTEPS + ROWS)),
    )
    if first:
        base = FSTEPS * m
        tails = [ref[base : base + BLOCK, :].astype(f32) for ref, _ in sources]
        tails = [jnp.where(is_odd == 1, tails[k], tails[3 - k]) for k in range(4)]
        speed = jnp.concatenate([x[:FSTEPS] for x in tails], axis=0)
        spread = jnp.concatenate([x[FSTEPS : 2 * FSTEPS] for x in tails], axis=0)
        coef_ref[0] = 1.0 - speed - 4.0 * spread
        coef_ref[1] = speed + spread
        coef_ref[2] = spread
        describe(m, me, sample_ref, cell_ref, value_ref, kind_ref, count_ref, std_ref)
    lane = lax.broadcasted_iota(jnp.int32, (8, LANES), 1)
    leftmost = lane == 0
    rightmost = lane == LANES - 1

    def block(i, carry):
        start = pl.multiple_of(i * BLOCK, BLOCK)
        for ref, first_row in sources:
            for r in range(FSTEPS):
                at = pl.multiple_of(r * m + start, BLOCK)
                even[first_row + r] = ref[pl.ds(at, BLOCK), :].astype(f32)
        source, target = even, odd
        for step in range(1, FSTEPS + 1):
            for half in range(0, BLOCK, 8):

                def row(r):
                    return [
                        source[r, half : half + 8, t * LANES : (t + 1) * LANES]
                        for t in range(tiles)
                    ]

                above, centre = row(step - 1), row(step)
                for r in range(step, total - step):
                    below = row(r + 1)
                    right = [pltpu.roll(c, 1, 1) for c in centre]
                    left = [pltpu.roll(c, LANES - 1, 1) for c in centre]
                    for t in range(tiles):
                        cut = slice(t * LANES, (t + 1) * LANES)
                        west = jnp.where(leftmost, right[t - 1] if t else 0.0, right[t])
                        east = jnp.where(
                            rightmost, left[t + 1] if t + 1 < tiles else 0.0, left[t]
                        )
                        target[r, half : half + 8, cut] = (
                            coef_ref[0, r : r + 1, cut] * centre[t]
                            + coef_ref[1, r : r + 1, cut] * above[t]
                            + coef_ref[2, r : r + 1, cut] * (below[t] + (west + east))
                        )
                    above, centre = centre, below
            source, target = target, source
        for t in range(tiles):
            cell = cell_ref[t : t + 1, :]
            at_row = jnp.broadcast_to(cell // LANES, (8, LANES))
            at_lane = jnp.broadcast_to(cell % LANES, (8, LANES))
            halves = []
            for half in range(0, BLOCK, 8):
                taken = jnp.zeros((8, LANES), f32)
                for y in range(ROWS):
                    values = source[
                        y + FSTEPS, half : half + 8, t * LANES : (t + 1) * LANES
                    ]
                    picked = jnp.take_along_axis(
                        values, at_lane, axis=1, mode="promise_in_bounds"
                    )
                    taken = jnp.where(at_row == y, picked, taken)
                halves.append(taken)
            at = pl.multiple_of(before + start, BLOCK)
            sample_ref[pl.ds(at, BLOCK), t * LANES : (t + 1) * LANES] = jnp.concatenate(
                halves, axis=0
            ).astype(bf16)
        for y in range(ROWS):
            field_ref[y, pl.ds(start, BLOCK), :] = source[y + FSTEPS].astype(bf16)
        return carry

    lax.fori_loop(0, m // BLOCK, block, 0)


def forecast(first, m, place, own, beside, cell, extra):
    width = own[0].shape[1]
    total = ROWS + 2 * FSTEPS
    outs = []
    if first:
        outs.append(jax.ShapeDtypeStruct((3, total, width), f32))
    rows = m + (BLOCK if first else extra[1].shape[0])
    outs.append(jax.ShapeDtypeStruct((rows, width), bf16))
    outs.append(jax.ShapeDtypeStruct((ROWS, m, width), bf16))
    args = (place,) + tuple(own) + tuple(beside) + (cell,) + tuple(extra)
    scratch = [pltpu.VMEM((total, BLOCK, width), f32)] * 2
    specs = [smem()] + [vmem()] * 5 + ([vmem()] * 2 + [smem()] * 2 if first else [vmem()] * 2)
    return call(
        functools.partial(forecast_kernel, first, m),
        outs,
        scratch,
        140 * 10**6 * m,
        args,
        specs,
    )


def reach_kernel(groups, place_ref, near_ref, own_ref, far_ref, *rest):
    parts, padded = rest[:-1], rest[-1]
    rows, width = own_ref.shape
    span = 2 * width // groups
    me, is_odd = place_ref[0], place_ref[1]
    facts = rows - BLOCK
    own = own_ref[facts:, :].astype(f32)
    for i, ref in ((1 - is_odd, near_ref), (is_odd, far_ref)):
        padded[i, :, :LANES] = jnp.zeros((rows, LANES), bf16)
        padded[i, :, LANES + width :] = jnp.zeros((rows, LANES), bf16)
        padded[i, :facts, LANES : LANES + width] = ref[:facts, :]
        padded[i, facts:, LANES : LANES + width] = jnp.concatenate(
            [ref[facts:, :].astype(f32)[:8], own[:8]], axis=0
        ).astype(bf16)
    for k, part in enumerate(parts):
        column = pl.multiple_of((me // 2 ^ k) * span, LANES)
        for i in range(2):
            part[i] = padded[i, :, pl.ds(column, span + 2 * LANES)]


def reached(groups, place, near, own, far):
    rows, width = own.shape
    wide = 2 * width // groups + 2 * LANES
    return call(
        functools.partial(reach_kernel, groups),
        [jax.ShapeDtypeStruct((2, rows, wide), bf16) for _ in range(groups // 2)],
        [pltpu.VMEM((2, rows, width + 2 * LANES), bf16)],
        0,
        (place, near, own, far),
        [smem()] + [vmem()] * 3,
    )


def merge_kernel(half, chunks, patches, place_ref, cell_ref, *rest):
    sample_refs = rest[:half]
    field_refs = rest[half : half + half * len(chunks)]
    mine, theirs, taken = rest[half + half * len(chunks) :]
    core = place_ref[0] % 2
    first = (place_ref[0] - core) * patches - 1
    strip = cell_ref.shape[0]
    tile_trials = sum(chunks)
    span = patches * LANES
    wide = span + 2 * LANES
    for t in range(2 * patches + 2):
        patch = jnp.clip(first + t, 0, strip - 1)
        cell = cell_ref[pl.ds(patch, 1), :]
        at_row = jnp.broadcast_to(cell // LANES, (8, LANES))
        at_lane = jnp.broadcast_to(cell % LANES, (8, LANES))
        column = pl.multiple_of(patch * LANES, LANES)
        at = 0
        for ref in field_refs:
            for k in range(0, ref.shape[1], BLOCK):
                picked = [jnp.zeros((8, LANES), f32), jnp.zeros((8, LANES), f32)]
                for y in range(ROWS):
                    entry = ref[y, k : k + BLOCK, pl.ds(column, LANES)].astype(f32)
                    here = at_row == y
                    for h in range(2):
                        values = jnp.take_along_axis(
                            entry[8 * h : 8 * h + 8],
                            at_lane,
                            axis=1,
                            mode="promise_in_bounds",
                        )
                        picked[h] = jnp.where(here, values, picked[h])
                taken[at : at + BLOCK, t * LANES : (t + 1) * LANES] = jnp.concatenate(
                    picked, axis=0
                ).astype(bf16)
                at += BLOCK
    for ref, column in ((mine, core * span), (theirs, (1 - core) * span)):
        cut = pl.ds(pl.multiple_of(column, LANES), wide)
        for k in range(half):
            at = 3 * k * tile_trials
            ref[at : at + tile_trials, :] = sample_refs[k][0, :tile_trials, cut]
            at += tile_trials
            ref[at : at + tile_trials, :] = taken[k * tile_trials : (k + 1) * tile_trials, cut]
            at += tile_trials
            ref[at : at + tile_trials, :] = sample_refs[k][1, :tile_trials, cut]
        for i in range(2):
            facts = sum(x[i, tile_trials:, cut].astype(f32) for x in sample_refs)
            at = 3 * half * tile_trials + i * BLOCK
            ref[at : at + BLOCK, :] = facts.astype(bf16)


def merged(chunks, patches, place, cell, samples, fields):
    half = len(samples)
    args = (place, cell) + tuple(samples) + tuple(fields)
    tile_trials = sum(chunks)
    shape = (3 * half * tile_trials + 2 * BLOCK, (patches + 2) * LANES)
    return call(
        functools.partial(merge_kernel, half, chunks, patches),
        [jax.ShapeDtypeStruct(shape, bf16)] * 2,
        [pltpu.VMEM((half * tile_trials, (2 * patches + 2) * LANES), bf16)],
        10**9,
        args,
        [smem()] + [vmem()] * (len(args) - 1),
    )


def product(a, b):
    return jnp.dot(a, b, preferred_element_type=f32)


def halves_of(a):
    high = a.astype(bf16)
    return high, (a - high.astype(f32)).astype(bf16)


def wide_product(a, b):
    return product(a[0], b[0]) + (product(a[0], b[1]) + product(a[1], b[0]))


def transform_kernel(groups, even_ref, odd_ref, *rest):
    outs = rest[:groups]
    values = rest[groups]
    _, members, width = values.shape
    wide = width // LANES
    patches = wide - 2
    tile_trials = members // groups
    for d in range(groups):
        ref = odd_ref if d % 2 else even_ref
        at = d * tile_trials
        for i in range(3):
            start = (3 * (d // 2) + i) * tile_trials
            values[i, at : at + tile_trials, :] = ref[start : start + tile_trials, :]
    last = 3 * (groups // 2) * tile_trials
    both = even_ref[last:, :].astype(f32) + odd_ref[last:, :].astype(f32)
    facts = (both[:BLOCK], both[BLOCK:])
    about = []
    for terms in (facts[0][:8], facts[0][8:], facts[1][:8]):
        about.append(
            (
                (terms[0:1] + terms[1:2]) + terms[2:3],
                (terms[3:4] + terms[4:5]) + terms[5:6],
                terms[6:7],
                terms[7:8],
            )
        )
    deviation = [[None] * wide for _ in range(3)]
    gap = [[None] * wide for _ in range(3)]
    for i in range(3):
        for t in range(wide):
            cut = slice(t * LANES, (t + 1) * LANES)
            entry = values[i, :, cut].astype(f32)
            average = jnp.sum(entry, axis=0, keepdims=True) * (1.0 / members)
            deviation[i][t] = entry - average
            gap[i][t] = about[i][0][:, cut] - average
    factor = float(members - 1)
    row_id = lax.broadcasted_iota(jnp.int32, (members, members), 0)
    col_id = lax.broadcasted_iota(jnp.int32, (members, members), 1)
    diagonal = row_id == col_id
    state = []
    for q in range(patches):
        pieces = []
        pull = jnp.zeros((members, LANES), f32)
        for i in range(3):
            for t in range(q, q + 3):
                cut = slice(t * LANES, (t + 1) * LANES)
                inverse = about[i][1][:, cut]
                cell_y = about[i][2][:, cut]
                cell_x = about[i][3][:, cut]
                off_y = ((i - 1) * ROWS + cell_y - (ROWS - 1) / 2.0) / ROWS
                off_x = ((t - q - 1) * LANES + cell_x - (LANES - 1) / 2.0) / LANES
                local = inverse * jnp.exp(-0.5 * off_y * off_y - 0.5 * off_x * off_x)
                weight = jnp.sqrt(local * (1.0 / factor))
                pieces.append((deviation[i][t] * weight).astype(bf16))
                pull = pull + deviation[i][t] * (local * (1.0 / factor) * gap[i][t])
        scaled = jnp.concatenate(pieces, axis=1)
        gram = lax.dot_general(
            scaled, scaled, (((1,), (1,)), ((), ())), preferred_element_type=f32
        )
        system = jnp.where(diagonal, gram + 1.0, gram)
        squared = jnp.sum(system * system, axis=0, keepdims=True)
        squared = jnp.sum(squared, axis=1, keepdims=True)
        scale = jnp.sqrt(squared)
        state.append([system * (1.0 / scale), None, scale, jnp.sum(pull, axis=1, keepdims=True)])
    for step in range(NSIT):
        fine = step >= NSIT - 2
        for s in state:
            w, z = s[0], s[1]
            if fine:
                half = halves_of(w * -0.5)
                mul = lambda a: wide_product(halves_of(a), half)
            else:
                half = (w * -0.5).astype(bf16)
                mul = lambda a: product(a.astype(bf16), half)
            if z is None:
                s[1] = jnp.where(diagonal, 1.5, 0.0) - 0.5 * w
            else:
                s[1] = 1.5 * z + mul(z)
            if step < NSIT - 1:
                between = 1.5 * w + mul(w)
                s[0] = 1.5 * between + mul(between)
    for q in range(patches):
        _, z, scale, pull = state[q]
        root = z * lax.rsqrt(scale)
        pull = jnp.sum(jnp.where(diagonal, pull, 0.0), axis=0, keepdims=True)
        once = jnp.sum(root * pull, axis=1, keepdims=True)
        gain = jnp.sum(root * once, axis=0, keepdims=True)
        middle = jnp.sum(root, axis=1, keepdims=True) * (1.0 / members)
        shift = gain - jnp.sum(gain, axis=1, keepdims=True) * (1.0 / members) + 1.0 / members
        mixing = ((root - middle) + shift).astype(bf16)
        for d in range(groups):
            outs[d][q] = mixing[d * tile_trials : (d + 1) * tile_trials, :]


def transform(groups, tile_trials, even, odd):
    wide = even.shape[1]
    members = groups * tile_trials
    return call(
        functools.partial(transform_kernel, groups),
        [
            jax.ShapeDtypeStruct((wide // LANES - 2, tile_trials, members), bf16)
            for _ in range(groups)
        ],
        [pltpu.VMEM((3, members, wide), bf16)],
        4 * 10**9,
        (even, odd),
        [vmem()] * 2,
    )


def analysis_kernel(groups, chunks, place_ref, *rest):
    mixing_refs = rest[:groups]
    count = groups * len(chunks)
    field_refs = rest[groups : groups + count]
    out_ref, turned = rest[groups + count :]
    patches, tile_trials, _ = mixing_refs[0].shape
    me = place_ref[0]
    for e in range(groups):
        for q in range(patches):
            column = pl.multiple_of(((me ^ e) * patches + q) * LANES, LANES)
            pieces = []
            for y in range(ROWS):
                stack = [
                    field_refs[j * groups + (k ^ e)][y, :, pl.ds(column, LANES)]
                    for k in range(groups)
                    for j in range(len(chunks))
                ]
                pieces.append(jnp.concatenate(stack, axis=0))
            result = product(mixing_refs[e][q], jnp.concatenate(pieces, axis=1))
            for y in range(ROWS):
                turned[pl.ds(y, tile_trials, stride=ROWS), :] = result[
                    :, y * LANES : (y + 1) * LANES
                ]
            out_ref[:, :, pl.ds(column, LANES)] = (
                turned[...].reshape(tile_trials, ROWS, LANES).astype(bf16)
            )


def analysed(groups, chunks, place, mixing, fields):
    tile_trials = sum(chunks)
    width = fields[0].shape[2]
    args = (place,) + tuple(mixing) + tuple(fields)
    return call(
        functools.partial(analysis_kernel, groups, chunks),
        [jax.ShapeDtypeStruct((tile_trials, ROWS, width), bf16)],
        [pltpu.VMEM((tile_trials * ROWS, LANES), f32)],
        2 * tile_trials * tile_trials * groups * ROWS * width,
        args,
        [smem()] + [vmem()] * (len(args) - 1),
    )[0]


def across(parts):
    groups = len(parts)
    out = list(parts)
    for d in sorted(range(1, groups), reverse=True):
        out[d] = lax.ppermute(parts[d], "cols", [(i, i ^ d) for i in range(groups)])
    return out


def everywhere(held, bits, groups):
    held = dict(held)
    for bit in bits:
        pairs = [(i, i ^ bit) for i in range(groups)]
        held.update({d ^ bit: lax.ppermute(x, "cols", pairs) for d, x in held.items()})
    return held


def after(x, other):
    return lax.optimization_barrier((x, other))[0]


def beside(to_near, to_far):
    count = lax.axis_size("rows")
    near = [(i, i ^ 1) for i in range(count) if i ^ 1 < count]
    far = [(i, i + 1) for i in range(1, count - 1, 2)]
    far += [(j, i) for i, j in far]
    return lax.ppermute(to_near, "rows", near), lax.ppermute(to_far, "rows", far)


def on_device(
    prior_trials, courant, diffusion, obs_cell, obs_count, obs_value, error_kind, error_std
):
    tile_trials = prior_trials.shape[0]
    groups = lax.axis_size("cols")
    place = jnp.stack([lax.axis_index("cols"), lax.axis_index("rows") % 2]).astype(jnp.int32)
    half = tile_trials // 2
    chunks = (half, half) if half % BLOCK == 0 else (tile_trials,)

    bits = [1 << k for k in reversed(range(groups.bit_length() - 1))]

    messages = packed(chunks, place, prior_trials, courant, diffusion)
    halos = []
    for j in range(len(chunks)):
        pair = messages[2 * j : 2 * j + 2]
        if j:
            pair, halos[j - 1] = lax.optimization_barrier((pair, halos[j - 1]))
        halos.append(beside(*pair))
    coef, sampled, fields = None, None, []
    for j, m in enumerate(chunks):
        extra = (obs_value, error_kind, obs_count, error_std) if j == 0 else (coef, sampled)
        made = forecast(
            j == 0, m, place, messages[2 * j : 2 * j + 2], halos[j], obs_cell[0], extra
        )
        if j == 0:
            coef, made = made[0], made[1:]
        sampled, field = made
        fields.append(everywhere({0: field}, bits[:-1], groups))
    near, far = beside(sampled, sampled)
    samples = list(reached(groups, place, near, sampled, far))
    for k in range(1, groups // 2):
        samples[k] = lax.ppermute(samples[k], "cols", [(i, i ^ 2 * k) for i in range(groups)])
    held = [field[d] for d in range(0, groups, 2) for field in fields]
    mine, theirs = merged(chunks, obs_count.shape[1], place, obs_cell[0], samples, held)
    theirs = lax.ppermute(theirs, "cols", [(i, i ^ 1) for i in range(groups)])
    mixing = transform(groups, tile_trials, mine, theirs)
    fields = [everywhere(after(field, mine), bits[-1:], groups) for field in fields]
    fields = [field[d] for field in fields for d in range(groups)]
    return analysed(groups, chunks, place, across(after(mixing, fields)), fields)


def solution(mesh):
    placed = (
        P("cols", "rows", None),
        P("rows", None),
        P("rows", None),
        P("rows", None, None),
        P("rows", "cols"),
        P("rows", "cols", None),
        P("rows", "cols", None),
        P(),
    )
    return jax.shard_map(
        on_device, mesh=mesh, in_specs=placed, out_specs=P("cols", "rows", None), check_vma=False
    )
```

time: 114 us -> 74 us (0.65)
  starting transfers between devices: 47.8 us -> 21.4 us
  local copies, waits for them, and re-layouts: 9.03 us -> 1.91 us
  Pallas kernels: 23.7 us -> 20.3 us
  waiting for transfers between devices: 31.3 us -> 29.8 us
    ppermute x15 -> x3, waiting for transfers between devices: 24.9 us -> 3.62 us  [across(): out[d] = lax.ppermute(parts[d], 'cols', [(i, i ^ d) for i in range(groups)])]
    ppermute x12 -> x14, waiting for transfers between devices: 6.41 us -> 26.2 us  [the longest x3 12 us: beside(): lax.ppermute(to_near, 'rows', near)]
    ppermute x12 -> x14, starting transfers between devices: 35.5 us -> 19.2 us  [the longest x3 10.3 us: beside(): lax.ppermute(to_far, 'rows', far)]
    ppermute x15 -> x3, starting transfers between devices: 12.3 us -> 2.23 us  [across(): out[d] = lax.ppermute(parts[d], 'cols', [(i, i ^ d) for i in range(groups)])]
    unnamed x73 -> x16, local copies, waits for them, and re-layouts: 8.15 us -> 1.91 us
    pallas_call x6 -> x7, Pallas kernels: 23.7 us -> 20.3 us  [call(): pl.pallas_call(kernel, out_shape=outs, in_specs=specs, out_specs=[vmem()...]
  transfers between devices with their start and end apart: 27 -> 17, of which waited for: 11 -> 8; matrix products, arithmetic and copies ran while one was open for 1% -> 0% of each run, Pallas kernels for 13% -> 20%
where the time goes in v2:
time: 74 us; the launch traced here: 73.6 us
  waiting for transfers between devices  29.8 us (40%)
  starting transfers between devices  21.4 us (29%)
  Pallas kernels  20.3 us (27%)
  local copies, waits for them, and re-layouts  1.91 us (3%)
    pallas_call x7, Pallas kernels, call(): pl.pallas_call(kernel, out_shape=outs, in_specs=specs, out_specs=[vmem()...  20.3 us
    ppermute x3, waiting for transfers between devices, beside(): lax.ppermute(to_near, 'rows', near)  12 us
    ppermute x3, starting transfers between devices, beside(): lax.ppermute(to_far, 'rows', far)  10.3 us
    ppermute x1, waiting for transfers between devices, on_device(): lax.ppermute(samples[k], 'cols', [(i, i ^ 2 * k) for i in range(groups)])  9.99 us
    ppermute x3, waiting for transfers between devices, beside(): lax.ppermute(to_far, 'rows', far)  3.74 us
    ppermute x6, starting transfers between devices, everywhere(): lax.ppermute(x, 'cols', pairs)  3.63 us
    ppermute x3, waiting for transfers between devices, across(): out[d] = lax.ppermute(parts[d], 'cols', [(i, i ^ d) for i in range(groups)])  3.62 us
    ppermute x1, starting transfers between devices, on_device(): theirs = lax.ppermute(theirs, 'cols', [(i, i ^ 1) for i in range(groups)])  3.09 us
  transfers between devices with their start and end apart: 17, of which 8 were waited for; matrix products, arithmetic and copies ran while one was open for 0% of the time, Pallas kernels for 20%

profile of v2, /device:TPU:11, one launch (start us, length us, event | category | flops | bytes accessed | tf_op | source)
XLA Modules:
  0.0 73.6 jit_solution(16682788098127019356)
XLA Ops:
  0.1 0.6 copy-done.1
  0.7 1.2 %copy-done = bf16[64,8,1024]{2,1,0:T(8,128)(2,1)S(1)} copy-done((bf16[64,8,1024]{2,1,0:T(8,128)(2,1)S(1)}, bf16[64,8,1024]{2,1,0:T(8,128)(2,1)}, u32[]{:S(2)}) %copy-start) | copy-done | bytes 1048600
  2.0 1.1 %shard_map.82 = (bf16[144,1024]{1,0:T(8,128)(2,1)S(1)}, bf16[144,1024]{1,0:T(8,128)(2,1)S(1)}, bf16[128,1024]{1,0:T(8,128)(2,1)S(1)}, bf16[128,1024]{1,0:T(8,128)(2,1)S(1)}) custom-call(s32[2]{0:T(128)S(1)} %pad_add_fusion.place_ref, bf16[64,8,1024]{2,1,0:T(8,128)(2,1)S(1)} %copy-done, bf16[8,1024]{1,0:T(8,128)(2,1)S(1)} %copy-done.1, ...), custom_call_target="tpu_custom_call" | custom-call | bytes 2195464 | tf_op jit(solution)/shard_map/pallas_call | solution.py:26
  3.4 4.1 %collective-permute-start.1 = (bf16[144,1024]{1,0:T(8,128)(2,1)S(1)}, bf16[144,1024]{1,0:T(8,128)(2,1)S(1)}, u32[]{:S(2)}, u32[]{:S(2)}) collective-permute-start(bf16[144,1024]{1,0:T(8,128)(2,1)S(1)} %get-tuple-element.37.far_ref), channel_id=1, source_target_pairs={{1,2},{3,4},{5,6},{2,1},{4,3},{6,5},{9,10},{11,12},{13,14},{10,9},... | collective-permute-start | bytes 884744 | tf_op jit(solution)/shard_map/ppermute | solution.py:528
  7.5 9.8 %collective-permute-done.from_near_ref = bf16[144,1024]{1,0:T(8,128)(2,1)S(1)} collective-permute-done((bf16[144,1024]{1,0:T(8,128)(2,1)S(1)}, bf16[144,1024]{1,0:T(8,128)(2,1)S(1)}, u32[]{:S(2)}, u32[]{:S(2)}) %collective-permute-start) | collective-permute-done | bytes 294944 | tf_op jit(solution)/shard_map/ppermute | solution.py:528
  17.7 4.1 %collective-permute-start.3 = (bf16[128,1024]{1,0:T(8,128)(2,1)S(1)}, bf16[128,1024]{1,0:T(8,128)(2,1)S(1)}, u32[]{:S(2)}, u32[]{:S(2)}) collective-permute-start(bf16[128,1024]{1,0:T(8,128)(2,1)S(1)} %get-tuple-element.39.far_ref), channel_id=1, source_target_pairs={{1,2},{3,4},{5,6},{2,1},{4,3},{6,5},{9,10},{11,12},{13,14},{10,9},... | collective-permute-start | bytes 786440 | tf_op jit(solution)/shard_map/ppermute | solution.py:528
  21.9 5.2 %shard_map.83 = (f32[3,16,1024]{2,1,0:T(8,128)S(1)}, bf16[48,1024]{1,0:T(8,128)(2,1)S(1)}, bf16[8,32,1024]{2,1,0:T(8,128)(2,1)S(1)}) custom-call(s32[2]{0:T(128)S(1)} %pad_add_fusion.place_ref, bf16[144,1024]{1,0:T(8,128)(2,1)S(1)} %get-tuple-element.36.near_ref, bf16[144,1024]{1,0:T(8,128)(2,1)S(1)} %get-tuple-element.37.far_ref, ...), custom_call_target="tpu_custom_call" | custom-call | flops 4480000000 | bytes 2005024 | tf_op jit(solution)/shard_map/pallas_call | solution.py:26
  27.0 1.3 %collective-permute-start.7 = (bf16[8,32,1024]{2,1,0:T(8,128)(2,1)S(1)}, bf16[8,32,1024]{2,1,0:T(8,128)(2,1)S(1)}, u32[]{:S(2)}, u32[]{:S(2)}) collective-permute-start(bf16[8,32,1024]{2,1,0:T(8,128)(2,1)S(1)} %get-tuple-element.55.rest_2_.rest_4_), channel_id=1, source_target_pairs={{0,16},{8,24},{16,0},{24,8},{1,17},{9,25},{17,1},{25,9},{2,18},{10... | collective-permute-start | bytes 1572872 | tf_op jit(solution)/shard_map/ppermute | solution.py:515
  28.3 1.0 %collective-permute-done.2.from_near_ref = bf16[128,1024]{1,0:T(8,128)(2,1)S(1)} collective-permute-done((bf16[128,1024]{1,0:T(8,128)(2,1)S(1)}, bf16[128,1024]{1,0:T(8,128)(2,1)S(1)}, u32[]{:S(2)}, u32[]{:S(2)}) %collective-permute-start.2) | collective-permute-done | bytes 262176 | tf_op jit(solution)/shard_map/ppermute | solution.py:528
  29.3 5.1 %shard_map.84 = (bf16[80,1024]{1,0:T(8,128)(2,1)S(1)}, bf16[8,32,1024]{2,1,0:T(8,128)(2,1)S(1)}) custom-call(s32[2]{0:T(128)S(1)} %pad_add_fusion.place_ref, bf16[128,1024]{1,0:T(8,128)(2,1)S(1)} %get-tuple-element.38.near_ref, bf16[128,1024]{1,0:T(8,128)(2,1)S(1)} %get-tuple-element.39.far_ref, bf16[128,1024]{1,0:T(8,128)(2,1)S(1)} %collective-permute-done.2.from_near_ref, ...), custom_call_target="tpu_custom_call" | custom-call | flops 4480000000 | bytes 2035720 | tf_op jit(solution)/shard_map/pallas_call | solution.py:26
  34.4 1.3 %collective-permute-start.8 = (bf16[8,32,1024]{2,1,0:T(8,128)(2,1)S(1)}, bf16[8,32,1024]{2,1,0:T(8,128)(2,1)S(1)}, u32[]{:S(2)}, u32[]{:S(2)}) collective-permute-start(bf16[8,32,1024]{2,1,0:T(8,128)(2,1)S(1)} %get-tuple-element.57.rest_3_.rest_8_), channel_id=1, source_target_pairs={{0,16},{8,24},{16,0},{24,8},{1,17},{9,25},{17,1},{25,9},{2,18},{10... | collective-permute-start | bytes 1572872 | tf_op jit(solution)/shard_map/ppermute | solution.py:515
  35.7 2.0 %collective-permute-start.5 = (bf16[80,1024]{1,0:T(8,128)(2,1)S(1)}, bf16[80,1024]{1,0:T(8,128)(2,1)S(1)}, u32[]{:S(2)}, u32[]{:S(2)}) collective-permute-start(bf16[80,1024]{1,0:T(8,128)(2,1)S(1)} %get-tuple-element.44.own_ref), channel_id=1, source_target_pairs={{1,2},{3,4},{5,6},{2,1},{4,3},{6,5},{9,10},{11,12},{13,14},{10,9},... | collective-permute-start | bytes 491528 | tf_op jit(solution)/shard_map/ppermute | solution.py:528
  37.7 1.3 %collective-permute-start.4 = (bf16[80,1024]{1,0:T(8,128)(2,1)S(1)}, bf16[80,1024]{1,0:T(8,128)(2,1)S(1)}, u32[]{:S(2)}, u32[]{:S(2)}) collective-permute-start(bf16[80,1024]{1,0:T(8,128)(2,1)S(1)} %get-tuple-element.44.own_ref), channel_id=1, source_target_pairs={{0,1},{1,0},{2,3},{3,2},{4,5},{5,4},{6,7},{7,6},{8,9},{9,8},{10,11... | collective-permute-start | bytes 491528 | tf_op jit(solution)/shard_map/ppermute | solution.py:528
  39.0 3.7 %collective-permute-done.5.far_ref = bf16[80,1024]{1,0:T(8,128)(2,1)S(1)} collective-permute-done((bf16[80,1024]{1,0:T(8,128)(2,1)S(1)}, bf16[80,1024]{1,0:T(8,128)(2,1)S(1)}, u32[]{:S(2)}, u32[]{:S(2)}) %collective-permute-start.5) | collective-permute-done | bytes 163872 | tf_op jit(solution)/shard_map/ppermute | solution.py:528
  42.7 1.3 %collective-permute-done.4.near_ref = bf16[80,1024]{1,0:T(8,128)(2,1)S(1)} collective-permute-done((bf16[80,1024]{1,0:T(8,128)(2,1)S(1)}, bf16[80,1024]{1,0:T(8,128)(2,1)S(1)}, u32[]{:S(2)}, u32[]{:S(2)}) %collective-permute-start.4) | collective-permute-done | bytes 163872 | tf_op jit(solution)/shard_map/ppermute | solution.py:528
  44.0 0.6 shard_map.85
  44.9 10.0 %collective-permute-done.6.rest_1_ = bf16[2,80,768]{2,1,0:T(8,128)(2,1)S(1)} collective-permute-done((bf16[2,80,768]{2,1,0:T(8,128)(2,1)S(1)}, bf16[2,80,768]{2,1,0:T(8,128)(2,1)S(1)}, u32[]{:S(2)}, u32[]{:S(2)}) %collective-permute-start.6) | collective-permute-done | bytes 245792 | tf_op jit(solution)/shard_map/ppermute | solution.py:562
  54.9 1.1 %shard_map.86 = (bf16[416,512]{1,0:T(8,128)(2,1)S(1)}, bf16[416,512]{1,0:T(8,128)(2,1)S(1)}) custom-call(s32[2]{0:T(128)S(1)} %pad_add_fusion.place_ref, s32[8,128]{1,0:T(8,128)S(1)} %bitcast.5, bf16[2,80,768]{2,1,0:T(8,128)(2,1)S(1)} %get-tuple-element.45.rest_0_, bf16[2,80,768]{2,1,0:T(8,128)(2,1)S(1)} %collective-permute-done.6.rest_1_, ...), custom_call_target="tpu_custom_call" | custom-call | flops 1000000000 | bytes 3444744 | tf_op jit(solution)/shard_map/pallas_call | solution.py:26
  56.0 3.1 %collective-permute-start.9 = (bf16[416,512]{1,0:T(8,128)(2,1)S(1)}, bf16[416,512]{1,0:T(8,128)(2,1)S(1)}, u32[]{:S(2)}, u32[]{:S(2)}) collective-permute-start(bf16[416,512]{1,0:T(8,128)(2,1)S(1)} %get-tuple-element.50), channel_id=1, source_target_pairs={{0,8},{8,0},{16,24},{24,16},{1,9},{9,1},{17,25},{25,17},{2,10},{10... | collective-permute-start | bytes 1277960 | tf_op jit(solution)/shard_map/ppermute | solution.py:565
  60.5 4.1 %shard_map.87 = (bf16[2,64,256]{2,1,0:T(8,128)(2,1)S(1)}, bf16[2,64,256]{2,1,0:T(8,128)(2,1)S(1)}, bf16[2,64,256]{2,1,0:T(8,128)(2,1)S(1)}, bf16[2,64,256]{2,1,0:T(8,128)(2,1)S(1)}) custom-call(bf16[416,512]{1,0:T(8,128)(2,1)S(1)} %get-tuple-element.49.even_ref, bf16[416,512]{1,0:T(8,128)(2,1)S(1)} %collective-permute-done.9.odd_ref), custom_call_target="tpu_custom_call" | custom-call | flops 4000000000 | bytes 1114112 | tf_op jit(solution)/shard_map/pallas_call | solution.py:26
  65.1 1.2 %collective-permute-start.15 = (bf16[2,64,256]{2,1,0:T(8,128)(2,1)S(1)}, bf16[2,64,256]{2,1,0:T(8,128)(2,1)S(1)}, u32[]{:S(2)}, u32[]{:S(2)}) collective-permute-start(bf16[2,64,256]{2,1,0:T(8,128)(2,1)S(1)} %get-tuple-element.61), channel_id=1, source_target_pairs={{0,16},{8,24},{16,0},{24,8},{1,17},{9,25},{17,1},{25,9},{2,18},{10... | collective-permute-start | bytes 196616 | tf_op jit(solution)/shard_map/ppermute | solution.py:507
  66.9 1.8 %collective-permute-done.15.rest_2_ = bf16[2,64,256]{2,1,0:T(8,128)(2,1)S(1)} collective-permute-done((bf16[2,64,256]{2,1,0:T(8,128)(2,1)S(1)}, bf16[2,64,256]{2,1,0:T(8,128)(2,1)S(1)}, u32[]{:S(2)}, u32[]{:S(2)}) %collective-permute-start.15) | collective-permute-done | bytes 65568 | tf_op jit(solution)/shard_map/ppermute | solution.py:507
  68.6 1.8 %collective-permute-done.16.rest_3_ = bf16[2,64,256]{2,1,0:T(8,128)(2,1)S(1)} collective-permute-done((bf16[2,64,256]{2,1,0:T(8,128)(2,1)S(1)}, bf16[2,64,256]{2,1,0:T(8,128)(2,1)S(1)}, u32[]{:S(2)}, u32[]{:S(2)}) %collective-permute-start.16) | collective-permute-done | bytes 65568 | tf_op jit(solution)/shard_map/ppermute | solution.py:507
  70.5 3.1 %shard_map.88 = bf16[64,8,1024]{2,1,0:T(8,128)(2,1)} custom-call(s32[2]{0:T(128)S(1)} %pad_add_fusion.place_ref, bf16[2,64,256]{2,1,0:T(8,128)(2,1)S(1)} %get-tuple-element.59.rest_0_, bf16[2,64,256]{2,1,0:T(8,128)(2,1)S(1)} %collective-permute-done.14.rest_1_, bf16[2,64,256]{2,1,0:T(8,128)(2,1)S(1)} %collective-permute-done.15.rest_2_, ...), custom_call_target="tpu_custom_call" | custom-call | flops 268435456 | bytes 5505032 | tf_op jit(solution)/shard_map/pallas_call | solution.py:26
  (34 shorter events, 3.5 us)
Async XLA Ops:
  0.0 0.7 copy-start.2
  0.7 1.2 %copy-start = (bf16[64,8,1024]{2,1,0:T(8,128)(2,1)S(1)}, bf16[64,8,1024]{2,1,0:T(8,128)(2,1)}, u32[]{:S(2)}) copy-start(bf16[64,8,1024]{2,1,0:T(8,128)(2,1)} %prior_ref.1) | copy-start | bytes 3145732
  3.1 18.8 %copy-start.3 = (s32[1,8,128]{2,1,0:T(8,128)S(1)}, s32[1,8,128]{2,1,0:T(8,128)}, u32[]{:S(2)}) copy-start(s32[1,8,128]{2,1,0:T(8,128)} %param.11) | copy-start | bytes 12292
  3.1 14.3 %collective-permute-start = (bf16[144,1024]{1,0:T(8,128)(2,1)S(1)}, bf16[144,1024]{1,0:T(8,128)(2,1)S(1)}, u32[]{:S(2)}, u32[]{:S(2)}) collective-permute-start(bf16[144,1024]{1,0:T(8,128)(2,1)S(1)} %get-tuple-element.36.near_ref), channel_id=1, source_target_pairs={{0,1},{1,0},{2,3},{3,2},{4,5},{5,4},{6,7},{7,6},{8,9},{9,8},{10,11... | collective-permute-start | bytes 884744 | tf_op jit(solution)/shard_map/ppermute | solution.py:528
  3.4 13.9 %collective-permute-start.1 = (bf16[144,1024]{1,0:T(8,128)(2,1)S(1)}, bf16[144,1024]{1,0:T(8,128)(2,1)S(1)}, u32[]{:S(2)}, u32[]{:S(2)}) collective-permute-start(bf16[144,1024]{1,0:T(8,128)(2,1)S(1)} %get-tuple-element.37.far_ref), channel_id=1, source_target_pairs={{1,2},{3,4},{5,6},{2,1},{4,3},{6,5},{9,10},{11,12},{13,14},{10,9},... | collective-permute-start | bytes 884744 | tf_op jit(solution)/shard_map/ppermute | solution.py:528
  17.3 4.5 %copy-start.5 = (s32[1,2,128]{2,1,0:T(2,128)S(1)}, s32[1,2,128]{2,1,0:T(2,128)}, u32[]{:S(2)}) copy-start(s32[1,2,128]{2,1,0:T(2,128)} %rest_1_.1) | copy-start | bytes 3076
  17.3 4.5 %copy-start.7 = (f32[4]{0:T(128)S(1)}, f32[4]{0:T(128)}, u32[]{:S(2)}) copy-start(f32[4]{0:T(128)} %rest_3_.1) | copy-start | bytes 52
  17.3 4.5 %copy-start.4 = (f32[1,2,128]{2,1,0:T(2,128)S(1)}, f32[1,2,128]{2,1,0:T(2,128)}, u32[]{:S(2)}) copy-start(f32[1,2,128]{2,1,0:T(2,128)} %rest_0_.1) | copy-start | bytes 3076
  17.3 4.5 %copy-start.6 = (s32[1,2]{1,0:T(1,128)S(1)}, s32[1,2]{1,0:T(1,128)}, u32[]{:S(2)}) copy-start(s32[1,2]{1,0:T(1,128)} %rest_2_.1) | copy-start | bytes 28
  17.4 11.9 %collective-permute-start.2 = (bf16[128,1024]{1,0:T(8,128)(2,1)S(1)}, bf16[128,1024]{1,0:T(8,128)(2,1)S(1)}, u32[]{:S(2)}, u32[]{:S(2)}) collective-permute-start(bf16[128,1024]{1,0:T(8,128)(2,1)S(1)} %get-tuple-element.38.near_ref), channel_id=1, source_target_pairs={{0,1},{1,0},{2,3},{3,2},{4,5},{5,4},{6,7},{7,6},{8,9},{9,8},{10,11... | collective-permute-start | bytes 786440 | tf_op jit(solution)/shard_map/ppermute | solution.py:528
  17.7 11.6 %collective-permute-start.3 = (bf16[128,1024]{1,0:T(8,128)(2,1)S(1)}, bf16[128,1024]{1,0:T(8,128)(2,1)S(1)}, u32[]{:S(2)}, u32[]{:S(2)}) collective-permute-start(bf16[128,1024]{1,0:T(8,128)(2,1)S(1)} %get-tuple-element.39.far_ref), channel_id=1, source_target_pairs={{1,2},{3,4},{5,6},{2,1},{4,3},{6,5},{9,10},{11,12},{13,14},{10,9},... | collective-permute-start | bytes 786440 | tf_op jit(solution)/shard_map/ppermute | solution.py:528
  27.0 17.9 %collective-permute-start.7 = (bf16[8,32,1024]{2,1,0:T(8,128)(2,1)S(1)}, bf16[8,32,1024]{2,1,0:T(8,128)(2,1)S(1)}, u32[]{:S(2)}, u32[]{:S(2)}) collective-permute-start(bf16[8,32,1024]{2,1,0:T(8,128)(2,1)S(1)} %get-tuple-element.55.rest_2_.rest_4_), channel_id=1, source_target_pairs={{0,16},{8,24},{16,0},{24,8},{1,17},{9,25},{17,1},{25,9},{2,18},{10... | collective-permute-start | bytes 1572872 | tf_op jit(solution)/shard_map/ppermute | solution.py:515
  34.4 20.5 %collective-permute-start.8 = (bf16[8,32,1024]{2,1,0:T(8,128)(2,1)S(1)}, bf16[8,32,1024]{2,1,0:T(8,128)(2,1)S(1)}, u32[]{:S(2)}, u32[]{:S(2)}) collective-permute-start(bf16[8,32,1024]{2,1,0:T(8,128)(2,1)S(1)} %get-tuple-element.57.rest_3_.rest_8_), channel_id=1, source_target_pairs={{0,16},{8,24},{16,0},{24,8},{1,17},{9,25},{17,1},{25,9},{2,18},{10... | collective-permute-start | bytes 1572872 | tf_op jit(solution)/shard_map/ppermute | solution.py:515
  35.7 7.1 %collective-permute-start.5 = (bf16[80,1024]{1,0:T(8,128)(2,1)S(1)}, bf16[80,1024]{1,0:T(8,128)(2,1)S(1)}, u32[]{:S(2)}, u32[]{:S(2)}) collective-permute-start(bf16[80,1024]{1,0:T(8,128)(2,1)S(1)} %get-tuple-element.44.own_ref), channel_id=1, source_target_pairs={{1,2},{3,4},{5,6},{2,1},{4,3},{6,5},{9,10},{11,12},{13,14},{10,9},... | collective-permute-start | bytes 491528 | tf_op jit(solution)/shard_map/ppermute | solution.py:528
  37.7 6.3 %collective-permute-start.4 = (bf16[80,1024]{1,0:T(8,128)(2,1)S(1)}, bf16[80,1024]{1,0:T(8,128)(2,1)S(1)}, u32[]{:S(2)}, u32[]{:S(2)}) collective-permute-start(bf16[80,1024]{1,0:T(8,128)(2,1)S(1)} %get-tuple-element.44.own_ref), channel_id=1, source_target_pairs={{0,1},{1,0},{2,3},{3,2},{4,5},{5,4},{6,7},{7,6},{8,9},{9,8},{10,11... | collective-permute-start | bytes 491528 | tf_op jit(solution)/shard_map/ppermute | solution.py:528
  44.6 10.3 %collective-permute-start.6 = (bf16[2,80,768]{2,1,0:T(8,128)(2,1)S(1)}, bf16[2,80,768]{2,1,0:T(8,128)(2,1)S(1)}, u32[]{:S(2)}, u32[]{:S(2)}) collective-permute-start(bf16[2,80,768]{2,1,0:T(8,128)(2,1)S(1)} %get-tuple-element.46), channel_id=1, source_target_pairs={{0,16},{8,24},{16,0},{24,8},{1,17},{9,25},{17,1},{25,9},{2,18},{10... | collective-permute-start | bytes 737288 | tf_op jit(solution)/shard_map/ppermute | solution.py:562
  56.0 4.5 %collective-permute-start.9 = (bf16[416,512]{1,0:T(8,128)(2,1)S(1)}, bf16[416,512]{1,0:T(8,128)(2,1)S(1)}, u32[]{:S(2)}, u32[]{:S(2)}) collective-permute-start(bf16[416,512]{1,0:T(8,128)(2,1)S(1)} %get-tuple-element.50), channel_id=1, source_target_pairs={{0,8},{8,0},{16,24},{24,16},{1,9},{9,1},{17,25},{25,17},{2,10},{10... | collective-permute-start | bytes 1277960 | tf_op jit(solution)/shard_map/ppermute | solution.py:565
  59.1 5.5 %collective-permute-start.10 = (bf16[8,32,1024]{2,1,0:T(8,128)(2,1)S(1)}, bf16[8,32,1024]{2,1,0:T(8,128)(2,1)S(1)}, u32[]{:S(2)}, u32[]{:S(2)}) collective-permute-start(bf16[8,32,1024]{2,1,0:T(8,128)(2,1)S(1)} %get-tuple-element.55.rest_2_.rest_4_), channel_id=1, source_target_pairs={{0,8},{8,0},{16,24},{24,16},{1,9},{9,1},{17,25},{25,17},{2,10},{10... | collective-permute-start | bytes 1572872 | tf_op jit(solution)/shard_map/ppermute | solution.py:515
  59.2 5.4 %collective-permute-start.11 = (bf16[8,32,1024]{2,1,0:T(8,128)(2,1)S(1)}, bf16[8,32,1024]{2,1,0:T(8,128)(2,1)S(1)}, u32[]{:S(2)}, u32[]{:S(2)}) collective-permute-start(bf16[8,32,1024]{2,1,0:T(8,128)(2,1)S(1)} %collective-permute-done.7.rest_4_.rest_6_), channel_id=1, source_target_pairs={{0,8},{8,0},{16,24},{24,16},{1,9},{9,1},{17,25},{25,17},{2,10},{10... | collective-permute-start | bytes 1572872 | tf_op jit(solution)/shard_map/ppermute | solution.py:515
  59.6 5.0 %collective-permute-start.12 = (bf16[8,32,1024]{2,1,0:T(8,128)(2,1)S(1)}, bf16[8,32,1024]{2,1,0:T(8,128)(2,1)S(1)}, u32[]{:S(2)}, u32[]{:S(2)}) collective-permute-start(bf16[8,32,1024]{2,1,0:T(8,128)(2,1)S(1)} %get-tuple-element.57.rest_3_.rest_8_), channel_id=1, source_target_pairs={{0,8},{8,0},{16,24},{24,16},{1,9},{9,1},{17,25},{25,17},{2,10},{10... | collective-permute-start | bytes 1572872 | tf_op jit(solution)/shard_map/ppermute | solution.py:515
  59.7 4.9 %collective-permute-start.13 = (bf16[8,32,1024]{2,1,0:T(8,128)(2,1)S(1)}, bf16[8,32,1024]{2,1,0:T(8,128)(2,1)S(1)}, u32[]{:S(2)}, u32[]{:S(2)}) collective-permute-start(bf16[8,32,1024]{2,1,0:T(8,128)(2,1)S(1)} %collective-permute-done.8.rest_5_.rest_10_), channel_id=1, source_target_pairs={{0,8},{8,0},{16,24},{24,16},{1,9},{9,1},{17,25},{25,17},{2,10},{10... | collective-permute-start | bytes 1572872 | tf_op jit(solution)/shard_map/ppermute | solution.py:515
  64.6 2.2 %collective-permute-start.14 = (bf16[2,64,256]{2,1,0:T(8,128)(2,1)S(1)}, bf16[2,64,256]{2,1,0:T(8,128)(2,1)S(1)}, u32[]{:S(2)}, u32[]{:S(2)}) collective-permute-start(bf16[2,64,256]{2,1,0:T(8,128)(2,1)S(1)} %get-tuple-element.60), channel_id=1, source_target_pairs={{0,8},{8,0},{16,24},{24,16},{1,9},{9,1},{17,25},{25,17},{2,10},{10... | collective-permute-start | bytes 196616 | tf_op jit(solution)/shard_map/ppermute | solution.py:507
  65.1 3.6 %collective-permute-start.15 = (bf16[2,64,256]{2,1,0:T(8,128)(2,1)S(1)}, bf16[2,64,256]{2,1,0:T(8,128)(2,1)S(1)}, u32[]{:S(2)}, u32[]{:S(2)}) collective-permute-start(bf16[2,64,256]{2,1,0:T(8,128)(2,1)S(1)} %get-tuple-element.61), channel_id=1, source_target_pairs={{0,16},{8,24},{16,0},{24,8},{1,17},{9,25},{17,1},{25,9},{2,18},{10... | collective-permute-start | bytes 196616 | tf_op jit(solution)/shard_map/ppermute | solution.py:507
  66.3 4.2 %collective-permute-start.16 = (bf16[2,64,256]{2,1,0:T(8,128)(2,1)S(1)}, bf16[2,64,256]{2,1,0:T(8,128)(2,1)S(1)}, u32[]{:S(2)}, u32[]{:S(2)}) collective-permute-start(bf16[2,64,256]{2,1,0:T(8,128)(2,1)S(1)} %get-tuple-element.62), channel_id=1, source_target_pairs={{0,24},{8,16},{16,8},{24,0},{1,25},{9,17},{17,9},{25,1},{2,26},{10... | collective-permute-start | bytes 196616 | tf_op jit(solution)/shard_map/ppermute | solution.py:507
  (1 other events, 0.7 us)

commit v3 on v2

--- a/solution.py
+++ b/solution.py
@@ -34,57 +34,59 @@
     )(*args)
 
 
-def pack_kernel(chunks, place_ref, prior_ref, speed_ref, spread_ref, *rest):
-    messages, flat = rest[:-1], rest[-1]
-    odd = place_ref[1]
+def pack_kernel(offset, m, me_ref, odd_ref, prior_ref, *rest):
+    flat = rest[-1]
+    if offset == 0:
+        speed_ref, spread_ref, cell_ref = rest[:3]
+        pair, cells_ref = rest[3:5], rest[5]
+        cells_ref[...] = cell_ref[...]
+    else:
+        pair = rest[:2]
+    odd = odd_ref[0]
 
     def fill(first_low, second_low):
-        offset = 0
-        for j, m in enumerate(chunks):
-            pair = messages[2 * j : 2 * j + 2]
-
-            def block(i, carry):
-                start = pl.multiple_of(i * BLOCK, BLOCK)
-                for t in range(flat.shape[0]):
-                    cut = slice(t * LANES, (t + 1) * LANES)
-                    entry = prior_ref[pl.ds(offset + start, BLOCK), :, cut].astype(f32)
-                    flat[t] = entry.reshape(BLOCK * ROWS, LANES)
-                    for ref, low in zip(pair, (first_low, second_low)):
-                        for r in range(FSTEPS):
-                            at = pl.multiple_of(r * m + start, BLOCK)
-                            ref[pl.ds(at, BLOCK), cut] = flat[
-                                t, pl.ds(low + r, BLOCK, stride=ROWS), :
-                            ].astype(bf16)
-                return carry
-
-            lax.fori_loop(0, m // BLOCK, block, 0)
-            if j == 0:
-                speed = speed_ref[...].astype(f32)
-                spread = spread_ref[...].astype(f32)
-                blank = jnp.zeros((BLOCK - 2 * FSTEPS, speed.shape[1]), f32)
+        def block(i, carry):
+            start = pl.multiple_of(i * BLOCK, BLOCK)
+            for t in range(flat.shape[0]):
+                cut = slice(t * LANES, (t + 1) * LANES)
+                entry = prior_ref[pl.ds(offset + start, BLOCK), :, cut].astype(f32)
+                flat[t] = entry.reshape(BLOCK * ROWS, LANES)
                 for ref, low in zip(pair, (first_low, second_low)):
-                    ref[FSTEPS * m :, :] = jnp.concatenate(
-                        [speed[low : low + FSTEPS], spread[low : low + FSTEPS], blank], axis=0
-                    ).astype(bf16)
-            offset += m
+                    for r in range(FSTEPS):
+                        at = pl.multiple_of(r * m + start, BLOCK)
+                        ref[pl.ds(at, BLOCK), cut] = flat[
+                            t, pl.ds(low + r, BLOCK, stride=ROWS), :
+                        ].astype(bf16)
+            return carry
+
+        lax.fori_loop(0, m // BLOCK, block, 0)
+        if offset == 0:
+            speed = speed_ref[...].astype(f32)
+            spread = spread_ref[...].astype(f32)
+            blank = jnp.zeros((BLOCK - 2 * FSTEPS, speed.shape[1]), f32)
+            for ref, low in zip(pair, (first_low, second_low)):
+                ref[FSTEPS * m :, :] = jnp.concatenate(
+                    [speed[low : low + FSTEPS], spread[low : low + FSTEPS], blank], axis=0
+                ).astype(bf16)
 
     pl.when(odd == 1)(lambda: fill(0, FSTEPS))
     pl.when(odd == 0)(lambda: fill(FSTEPS, 0))
 
 
-def packed(chunks, place, prior, speed, spread):
+def packed(offset, m, place, prior, extra):
     width = prior.shape[2]
-    outs = []
-    for j, m in enumerate(chunks):
-        rows = FSTEPS * m + (BLOCK if j == 0 else 0)
-        outs += [jax.ShapeDtypeStruct((rows, width), bf16)] * 2
+    rows = FSTEPS * m + (BLOCK if offset == 0 else 0)
+    outs = [jax.ShapeDtypeStruct((rows, width), bf16)] * 2
+    if offset == 0:
+        outs.append(jax.ShapeDtypeStruct(extra[2].shape, extra[2].dtype))
+    args = place + (prior,) + tuple(extra)
     return call(
-        functools.partial(pack_kernel, chunks),
+        functools.partial(pack_kernel, offset, m),
         outs,
         [pltpu.VMEM((width // LANES, BLOCK * ROWS, LANES), f32)],
         0,
-        (place, prior, speed, spread),
-        [smem()] + [vmem()] * 3,
+        args,
+        [smem()] * 2 + [vmem()] * (len(args) - 2),
     )
 
 
@@ -117,7 +119,7 @@
 
 
 def forecast_kernel(
-    first, m, place_ref, near_ref, far_ref, from_near_ref, from_far_ref, cell_ref, *rest
+    first, m, me_ref, odd_ref, near_ref, far_ref, from_near_ref, from_far_ref, cell_ref, *rest
 ):
     if first:
         value_ref, kind_ref, count_ref, std_ref, coef_ref, sample_ref = rest[:6]
@@ -133,7 +135,7 @@
     width = near_ref.shape[1]
     tiles = width // LANES
     total = ROWS + 2 * FSTEPS
-    me, is_odd = place_ref[0], place_ref[1]
+    me, is_odd = me_ref[0], odd_ref[0]
     sources = (
         (from_near_ref, (1 - is_odd) * (FSTEPS + ROWS)),
         (near_ref, FSTEPS + (1 - is_odd) * FSTEPS),
@@ -224,9 +226,9 @@
     rows = m + (BLOCK if first else extra[1].shape[0])
     outs.append(jax.ShapeDtypeStruct((rows, width), bf16))
     outs.append(jax.ShapeDtypeStruct((ROWS, m, width), bf16))
-    args = (place,) + tuple(own) + tuple(beside) + (cell,) + tuple(extra)
+    args = place + tuple(own) + tuple(beside) + (cell,) + tuple(extra)
     scratch = [pltpu.VMEM((total, BLOCK, width), f32)] * 2
-    specs = [smem()] + [vmem()] * 5 + ([vmem()] * 2 + [smem()] * 2 if first else [vmem()] * 2)
+    specs = [smem()] * 2 + [vmem()] * 5 + ([vmem()] * 2 + [smem()] * 2 if first else [vmem()] * 2)
     return call(
         functools.partial(forecast_kernel, first, m),
         outs,
@@ -237,11 +239,11 @@
     )
 
 
-def reach_kernel(groups, place_ref, near_ref, own_ref, far_ref, *rest):
+def reach_kernel(groups, me_ref, odd_ref, near_ref, own_ref, far_ref, *rest):
     parts, padded = rest[:-1], rest[-1]
     rows, width = own_ref.shape
     span = 2 * width // groups
-    me, is_odd = place_ref[0], place_ref[1]
+    me, is_odd = me_ref[0], odd_ref[0]
     facts = rows - BLOCK
     own = own_ref[facts:, :].astype(f32)
     for i, ref in ((1 - is_odd, near_ref), (is_odd, far_ref)):
@@ -265,21 +267,15 @@
         [jax.ShapeDtypeStruct((2, rows, wide), bf16) for _ in range(groups // 2)],
         [pltpu.VMEM((2, rows, width + 2 * LANES), bf16)],
         0,
-        (place, near, own, far),
-        [smem()] + [vmem()] * 3,
-    )
-
-
-def merge_kernel(half, chunks, patches, place_ref, cell_ref, *rest):
-    sample_refs = rest[:half]
-    field_refs = rest[half : half + half * len(chunks)]
-    mine, theirs, taken = rest[half + half * len(chunks) :]
-    core = place_ref[0] % 2
-    first = (place_ref[0] - core) * patches - 1
+        place + (near, own, far),
+        [smem()] * 2 + [vmem()] * 3,
+    )
+
+
+def take_kernel(patches, me_ref, odd_ref, cell_ref, *rest):
+    field_refs, taken = rest[:-1], rest[-1]
+    first = me_ref[0] // 2 * 2 * patches - 1
     strip = cell_ref.shape[0]
-    tile_trials = sum(chunks)
-    span = patches * LANES
-    wide = span + 2 * LANES
     for t in range(2 * patches + 2):
         patch = jnp.clip(first + t, 0, strip - 1)
         cell = cell_ref[pl.ds(patch, 1), :]
@@ -305,6 +301,28 @@
                     picked, axis=0
                 ).astype(bf16)
                 at += BLOCK
+
+
+def taken_here(patches, place, cell, fields):
+    members = sum(x.shape[1] for x in fields)
+    args = place + (cell,) + tuple(fields)
+    return call(
+        functools.partial(take_kernel, patches),
+        [jax.ShapeDtypeStruct((members, (2 * patches + 2) * LANES), bf16)],
+        [],
+        10**9,
+        args,
+        [smem()] * 2 + [vmem()] * (len(args) - 2),
+    )[0]
+
+
+def merge_kernel(half, me_ref, odd_ref, taken, *rest):
+    sample_refs = rest[:half]
+    mine, theirs = rest[half:]
+    core = me_ref[0] % 2
+    tile_trials = taken.shape[0] // half
+    wide = mine.shape[1]
+    span = wide - 2 * LANES
     for ref, column in ((mine, core * span), (theirs, (1 - core) * span)):
         cut = pl.ds(pl.multiple_of(column, LANES), wide)
         for k in range(half):
@@ -320,18 +338,17 @@
             ref[at : at + BLOCK, :] = facts.astype(bf16)
 
 
-def merged(chunks, patches, place, cell, samples, fields):
+def merged(place, taken, samples):
     half = len(samples)
-    args = (place, cell) + tuple(samples) + tuple(fields)
-    tile_trials = sum(chunks)
-    shape = (3 * half * tile_trials + 2 * BLOCK, (patches + 2) * LANES)
+    shape = (3 * taken.shape[0] + 2 * BLOCK, taken.shape[1] // 2 + LANES)
+    args = place + (taken,) + tuple(samples)
     return call(
-        functools.partial(merge_kernel, half, chunks, patches),
+        functools.partial(merge_kernel, half),
         [jax.ShapeDtypeStruct(shape, bf16)] * 2,
-        [pltpu.VMEM((half * tile_trials, (2 * patches + 2) * LANES), bf16)],
-        10**9,
+        [],
+        0,
         args,
-        [smem()] + [vmem()] * (len(args) - 1),
+        [smem()] * 2 + [vmem()] * (len(args) - 2),
     )
 
 
@@ -458,14 +475,15 @@
     )
 
 
-def analysis_kernel(groups, chunks, place_ref, *rest):
-    mixing_refs = rest[:groups]
+def analysis_kernel(groups, chunks, turns, me_ref, odd_ref, *rest):
+    mixing_refs = rest[: len(turns)]
     count = groups * len(chunks)
-    field_refs = rest[groups : groups + count]
-    out_ref, turned = rest[groups + count :]
+    field_refs = rest[len(turns) : len(turns) + count]
+    out_ref, ready, turned, sems = rest[-4:]
     patches, tile_trials, _ = mixing_refs[0].shape
-    me = place_ref[0]
-    for e in range(groups):
+    me = me_ref[0]
+    copies = []
+    for e, mixing_ref in zip(turns, mixing_refs):
         for q in range(patches):
             column = pl.multiple_of(((me ^ e) * patches + q) * LANES, LANES)
             pieces = []
@@ -476,28 +494,49 @@
                     for j in range(len(chunks))
                 ]
                 pieces.append(jnp.concatenate(stack, axis=0))
-            result = product(mixing_refs[e][q], jnp.concatenate(pieces, axis=1))
+            result = product(mixing_ref[q], jnp.concatenate(pieces, axis=1))
+            at = len(copies)
             for y in range(ROWS):
-                turned[pl.ds(y, tile_trials, stride=ROWS), :] = result[
+                turned[at % 2, pl.ds(y, tile_trials, stride=ROWS), :] = result[
                     :, y * LANES : (y + 1) * LANES
                 ]
-            out_ref[:, :, pl.ds(column, LANES)] = (
-                turned[...].reshape(tile_trials, ROWS, LANES).astype(bf16)
+            ready[at] = turned[at % 2].reshape(tile_trials, ROWS, LANES).astype(bf16)
+            copy = pltpu.make_async_copy(
+                ready.at[at], out_ref.at[:, :, pl.ds(column, LANES)], sems.at[at]
             )
-
-
-def analysed(groups, chunks, place, mixing, fields):
-    tile_trials = sum(chunks)
+            copy.start()
+            copies.append(copy)
+    for copy in copies:
+        copy.wait()
+
+
+def analysed(groups, chunks, turns, place, mixing, fields, begun):
+    patches, tile_trials, _ = mixing[0].shape
     width = fields[0].shape[2]
-    args = (place,) + tuple(mixing) + tuple(fields)
-    return call(
-        functools.partial(analysis_kernel, groups, chunks),
-        [jax.ShapeDtypeStruct((tile_trials, ROWS, width), bf16)],
-        [pltpu.VMEM((tile_trials * ROWS, LANES), f32)],
-        2 * tile_trials * tile_trials * groups * ROWS * width,
-        args,
-        [smem()] + [vmem()] * (len(args) - 1),
-    )[0]
+    args = place + tuple(mixing[e] for e in turns) + tuple(fields)
+    specs = [smem()] * 2 + [vmem()] * (len(args) - 2)
+    aliases = {}
+    if begun is not None:
+        aliases = {len(args): 0}
+        args += (begun,)
+        specs.append(pl.BlockSpec(memory_space=pl.ANY))
+    out = jax.ShapeDtypeStruct((tile_trials, ROWS, width), bf16)
+    count = len(turns) * patches
+    moved = sum(x.size * x.dtype.itemsize for x in args) + 3 * out.size * 2
+    return pl.pallas_call(
+        functools.partial(analysis_kernel, groups, chunks, turns),
+        out_shape=out,
+        in_specs=specs,
+        out_specs=pl.BlockSpec(memory_space=pl.ANY),
+        scratch_shapes=[
+            pltpu.VMEM((count, tile_trials, ROWS, LANES), bf16),
+            pltpu.VMEM((2, tile_trials * ROWS, LANES), f32),
+            pltpu.SemaphoreType.DMA((count,)),
+        ],
+        input_output_aliases=aliases,
+        compiler_params=pltpu.CompilerParams(vmem_limit_bytes=moved + SLACK),
+        cost_estimate=pl.CostEstimate(flops=10**9, bytes_accessed=moved, transcendentals=0),
+    )(*args)
 
 
 def across(parts):
@@ -533,24 +572,27 @@
 ):
     tile_trials = prior_trials.shape[0]
     groups = lax.axis_size("cols")
-    place = jnp.stack([lax.axis_index("cols"), lax.axis_index("rows") % 2]).astype(jnp.int32)
+    place = (lax.axis_index("cols")[None], (lax.axis_index("rows") % 2)[None])
     half = tile_trials // 2
     chunks = (half, half) if half % BLOCK == 0 else (tile_trials,)
 
     bits = [1 << k for k in reversed(range(groups.bit_length() - 1))]
 
-    messages = packed(chunks, place, prior_trials, courant, diffusion)
-    halos = []
-    for j in range(len(chunks)):
-        pair = messages[2 * j : 2 * j + 2]
-        if j:
-            pair, halos[j - 1] = lax.optimization_barrier((pair, halos[j - 1]))
-        halos.append(beside(*pair))
+    messages, halos = [], []
+    for j, m in enumerate(chunks):
+        extra = () if j else (courant, diffusion, obs_cell[0])
+        made = packed(sum(chunks[:j]), m, place, prior_trials, extra)
+        if j == 0:
+            made, cells = made[:2], made[2]
+        else:
+            made, halos[j - 1] = lax.optimization_barrier((made, halos[j - 1]))
+        messages += made
+        halos.append(beside(*made))
     coef, sampled, fields = None, None, []
     for j, m in enumerate(chunks):
         extra = (obs_value, error_kind, obs_count, error_std) if j == 0 else (coef, sampled)
         made = forecast(
-            j == 0, m, place, messages[2 * j : 2 * j + 2], halos[j], obs_cell[0], extra
+            j == 0, m, place, messages[2 * j : 2 * j + 2], halos[j], cells, extra
         )
         if j == 0:
             coef, made = made[0], made[1:]
@@ -561,12 +603,15 @@
     for k in range(1, groups // 2):
         samples[k] = lax.ppermute(samples[k], "cols", [(i, i ^ 2 * k) for i in range(groups)])
     held = [field[d] for d in range(0, groups, 2) for field in fields]
-    mine, theirs = merged(chunks, obs_count.shape[1], place, obs_cell[0], samples, held)
+    taken = taken_here(obs_count.shape[1], place, cells, held)
+    mine, theirs = merged(place, taken, samples)
     theirs = lax.ppermute(theirs, "cols", [(i, i ^ 1) for i in range(groups)])
     mixing = transform(groups, tile_trials, mine, theirs)
     fields = [everywhere(after(field, mine), bits[-1:], groups) for field in fields]
     fields = [field[d] for field in fields for d in range(groups)]
-    return analysed(groups, chunks, place, across(after(mixing, fields)), fields)
+    mixing = across(after(mixing, fields))
+    begun = analysed(groups, chunks, (0, 1), place, mixing, fields, None)
+    return analysed(groups, chunks, tuple(range(2, groups)), place, mixing, fields, begun)
 
 
 def solution(mesh):

time: 74 us -> 69.9 us (0.945)
  Pallas kernels: 20.3 us -> 16.9 us
    pallas_call x7 -> x8, Pallas kernels: 20.3 us -> 13.8 us  [call(): pl.pallas_call(kernel, out_shape=outs, in_specs=specs, out_specs=[vmem()...]
    ppermute x6, waiting for transfers between devices: 0.02 us -> 5.77 us  [everywhere(): lax.ppermute(x, 'cols', pairs)]
    ppermute x1, waiting for transfers between devices: 9.99 us -> 4.76 us  [on_device(): lax.ppermute(samples[k], 'cols', [(i, i ^ 2 * k) for i in range(groups)])]
    pallas_call x0 -> x2, Pallas kernels: none -> 3.08 us  [analysed(): pl.pallas_call(functools.partial(analysis_kernel, groups, chunks, turns),...]
    ppermute x3, waiting for transfers between devices: 3.62 us -> 2.07 us  [across(): out[d] = lax.ppermute(parts[d], 'cols', [(i, i ^ d) for i in range(groups)])]
    unnamed x16 -> x18, local copies, waits for them, and re-layouts: 1.91 us -> 1.98 us
  transfers between devices with their start and end apart: 17 -> 17, of which waited for: 8 -> 9; matrix products, arithmetic and copies ran while one was open for 0% -> 0% of each run, Pallas kernels for 20% -> 22%
where the time goes in v3:
time: 69.9 us; the launch traced here: 69.6 us
  waiting for transfers between devices  29.1 us (42%)
  starting transfers between devices  21.4 us (31%)
  Pallas kernels  16.9 us (24%)
  local copies, waits for them, and re-layouts  1.98 us (3%)
    pallas_call x8, Pallas kernels, call(): pl.pallas_call(kernel, out_shape=outs, in_specs=specs, out_specs=[vmem()...  13.8 us
    ppermute x3, waiting for transfers between devices, beside(): lax.ppermute(to_near, 'rows', near)  12.4 us
    ppermute x3, starting transfers between devices, beside(): lax.ppermute(to_far, 'rows', far)  10.3 us
    ppermute x6, waiting for transfers between devices, everywhere(): lax.ppermute(x, 'cols', pairs)  5.77 us
    ppermute x1, waiting for transfers between devices, on_device(): lax.ppermute(samples[k], 'cols', [(i, i ^ 2 * k) for i in range(groups)])  4.76 us
    ppermute x3, waiting for transfers between devices, beside(): lax.ppermute(to_far, 'rows', far)  3.74 us
    ppermute x6, starting transfers between devices, everywhere(): lax.ppermute(x, 'cols', pairs)  3.63 us
    ppermute x1, starting transfers between devices, on_device(): theirs = lax.ppermute(theirs, 'cols', [(i, i ^ 1) for i in range(groups)])  3.1 us
  transfers between devices with their start and end apart: 17, of which 9 were waited for; matrix products, arithmetic and copies ran while one was open for 0% of the time, Pallas kernels for 22%

profile of v3, /device:TPU:11, one launch (start us, length us, event | category | flops | bytes accessed | tf_op | source)
XLA Modules:
  0.0 69.6 jit_solution(12765947183383632656)
XLA Ops:
  0.0 0.7 copy-done.4
  0.8 1.2 %copy-done = bf16[64,8,1024]{2,1,0:T(8,128)(2,1)S(1)} copy-done((bf16[64,8,1024]{2,1,0:T(8,128)(2,1)S(1)}, bf16[64,8,1024]{2,1,0:T(8,128)(2,1)}, u32[]{:S(2)}) %copy-start) | copy-done | bytes 1048600
  2.6 4.1 %collective-permute-start.1 = (bf16[144,1024]{1,0:T(8,128)(2,1)S(1)}, bf16[144,1024]{1,0:T(8,128)(2,1)S(1)}, u32[]{:S(2)}, u32[]{:S(2)}) collective-permute-start(bf16[144,1024]{1,0:T(8,128)(2,1)S(1)} %get-tuple-element.37.far_ref), channel_id=1, source_target_pairs={{1,2},{3,4},{5,6},{2,1},{4,3},{6,5},{9,10},{11,12},{13,14},{10,9},... | collective-permute-start | bytes 884744 | tf_op jit(solution)/shard_map/ppermute | solution.py:567
  7.0 9.5 %collective-permute-done.from_near_ref = bf16[144,1024]{1,0:T(8,128)(2,1)S(1)} collective-permute-done((bf16[144,1024]{1,0:T(8,128)(2,1)S(1)}, bf16[144,1024]{1,0:T(8,128)(2,1)S(1)}, u32[]{:S(2)}, u32[]{:S(2)}) %collective-permute-start) | collective-permute-done | bytes 294944 | tf_op jit(solution)/shard_map/ppermute | solution.py:567
  16.9 4.1 %collective-permute-start.3 = (bf16[128,1024]{1,0:T(8,128)(2,1)S(1)}, bf16[128,1024]{1,0:T(8,128)(2,1)S(1)}, u32[]{:S(2)}, u32[]{:S(2)}) collective-permute-start(bf16[128,1024]{1,0:T(8,128)(2,1)S(1)} %get-tuple-element.44.far_ref), channel_id=1, source_target_pairs={{1,2},{3,4},{5,6},{2,1},{4,3},{6,5},{9,10},{11,12},{13,14},{10,9},... | collective-permute-start | bytes 786440 | tf_op jit(solution)/shard_map/ppermute | solution.py:567
  21.0 4.6 %shard_map.84 = (f32[3,16,1024]{2,1,0:T(8,128)S(1)}, bf16[48,1024]{1,0:T(8,128)(2,1)S(1)}, bf16[8,32,1024]{2,1,0:T(8,128)(2,1)S(1)}) custom-call(s32[1]{0:T(128)} %bitcast.me_ref, s32[1]{0:T(128)} %bitcast.1.odd_ref, bf16[144,1024]{1,0:T(8,128)(2,1)S(1)} %get-tuple-element.36.near_ref, bf16[144,1024]{1,0:T(8,128)(2,1)S(1)} %get-tuple-element.37.far_ref, ...), custom_call_target="tpu_custom_call" | custom-call | flops 4480000000 | bytes 2005024 | tf_op jit(solution)/shard_map/pallas_call | solution.py:26
  25.6 1.3 %collective-permute-start.4 = (bf16[8,32,1024]{2,1,0:T(8,128)(2,1)S(1)}, bf16[8,32,1024]{2,1,0:T(8,128)(2,1)S(1)}, u32[]{:S(2)}, u32[]{:S(2)}) collective-permute-start(bf16[8,32,1024]{2,1,0:T(8,128)(2,1)S(1)} %get-tuple-element.57.rest_0_.rest_2_), channel_id=1, source_target_pairs={{0,16},{8,24},{16,0},{24,8},{1,17},{9,25},{17,1},{25,9},{2,18},{10... | collective-permute-start | bytes 1572872 | tf_op jit(solution)/shard_map/ppermute | solution.py:554
  26.9 1.6 %collective-permute-done.2.from_near_ref = bf16[128,1024]{1,0:T(8,128)(2,1)S(1)} collective-permute-done((bf16[128,1024]{1,0:T(8,128)(2,1)S(1)}, bf16[128,1024]{1,0:T(8,128)(2,1)S(1)}, u32[]{:S(2)}, u32[]{:S(2)}) %collective-permute-start.2) | collective-permute-done | bytes 262176 | tf_op jit(solution)/shard_map/ppermute | solution.py:567
  28.5 4.0 %shard_map.85 = (bf16[80,1024]{1,0:T(8,128)(2,1)S(1)}, bf16[8,32,1024]{2,1,0:T(8,128)(2,1)S(1)}) custom-call(s32[1]{0:T(128)} %bitcast.me_ref, s32[1]{0:T(128)} %bitcast.1.odd_ref, bf16[128,1024]{1,0:T(8,128)(2,1)S(1)} %get-tuple-element.43.near_ref, bf16[128,1024]{1,0:T(8,128)(2,1)S(1)} %get-tuple-element.44.far_ref, ...), custom_call_target="tpu_custom_call" | custom-call | flops 4480000000 | bytes 2035720 | tf_op jit(solution)/shard_map/pallas_call | solution.py:26
  32.5 1.3 %collective-permute-start.5 = (bf16[8,32,1024]{2,1,0:T(8,128)(2,1)S(1)}, bf16[8,32,1024]{2,1,0:T(8,128)(2,1)S(1)}, u32[]{:S(2)}, u32[]{:S(2)}) collective-permute-start(bf16[8,32,1024]{2,1,0:T(8,128)(2,1)S(1)} %get-tuple-element.59.rest_1_.rest_6_), channel_id=1, source_target_pairs={{0,16},{8,24},{16,0},{24,8},{1,17},{9,25},{17,1},{25,9},{2,18},{10... | collective-permute-start | bytes 1572872 | tf_op jit(solution)/shard_map/ppermute | solution.py:554
  33.8 2.0 %collective-permute-start.7 = (bf16[80,1024]{1,0:T(8,128)(2,1)S(1)}, bf16[80,1024]{1,0:T(8,128)(2,1)S(1)}, u32[]{:S(2)}, u32[]{:S(2)}) collective-permute-start(bf16[80,1024]{1,0:T(8,128)(2,1)S(1)} %get-tuple-element.48.own_ref), channel_id=1, source_target_pairs={{1,2},{3,4},{5,6},{2,1},{4,3},{6,5},{9,10},{11,12},{13,14},{10,9},... | collective-permute-start | bytes 491528 | tf_op jit(solution)/shard_map/ppermute | solution.py:567
  35.8 1.3 %collective-permute-start.6 = (bf16[80,1024]{1,0:T(8,128)(2,1)S(1)}, bf16[80,1024]{1,0:T(8,128)(2,1)S(1)}, u32[]{:S(2)}, u32[]{:S(2)}) collective-permute-start(bf16[80,1024]{1,0:T(8,128)(2,1)S(1)} %get-tuple-element.48.own_ref), channel_id=1, source_target_pairs={{0,1},{1,0},{2,3},{3,2},{4,5},{5,4},{6,7},{7,6},{8,9},{9,8},{10,11... | collective-permute-start | bytes 491528 | tf_op jit(solution)/shard_map/ppermute | solution.py:567
  37.1 3.7 %collective-permute-done.7.far_ref = bf16[80,1024]{1,0:T(8,128)(2,1)S(1)} collective-permute-done((bf16[80,1024]{1,0:T(8,128)(2,1)S(1)}, bf16[80,1024]{1,0:T(8,128)(2,1)S(1)}, u32[]{:S(2)}, u32[]{:S(2)}) %collective-permute-start.7) | collective-permute-done | bytes 163872 | tf_op jit(solution)/shard_map/ppermute | solution.py:567
  40.8 1.3 %collective-permute-done.6.near_ref = bf16[80,1024]{1,0:T(8,128)(2,1)S(1)} collective-permute-done((bf16[80,1024]{1,0:T(8,128)(2,1)S(1)}, bf16[80,1024]{1,0:T(8,128)(2,1)S(1)}, u32[]{:S(2)}, u32[]{:S(2)}) %collective-permute-start.6) | collective-permute-done | bytes 163872 | tf_op jit(solution)/shard_map/ppermute | solution.py:567
  42.5 5.8 %collective-permute-done.5.rest_3_.rest_8_ = bf16[8,32,1024]{2,1,0:T(8,128)(2,1)S(1)} collective-permute-done((bf16[8,32,1024]{2,1,0:T(8,128)(2,1)S(1)}, bf16[8,32,1024]{2,1,0:T(8,128)(2,1)S(1)}, u32[]{:S(2)}, u32[]{:S(2)}) %collective-permute-start.5) | collective-permute-done | bytes 524320 | tf_op jit(solution)/shard_map/ppermute | solution.py:554
  48.2 0.5 shard_map.86.taken
  48.7 4.8 %collective-permute-done.8.rest_1_ = bf16[2,80,768]{2,1,0:T(8,128)(2,1)S(1)} collective-permute-done((bf16[2,80,768]{2,1,0:T(8,128)(2,1)S(1)}, bf16[2,80,768]{2,1,0:T(8,128)(2,1)S(1)}, u32[]{:S(2)}, u32[]{:S(2)}) %collective-permute-start.8) | collective-permute-done | bytes 245792 | tf_op jit(solution)/shard_map/ppermute | solution.py:604
  53.5 3.1 %collective-permute-start.9 = (bf16[416,512]{1,0:T(8,128)(2,1)S(1)}, bf16[416,512]{1,0:T(8,128)(2,1)S(1)}, u32[]{:S(2)}, u32[]{:S(2)}) collective-permute-start(bf16[416,512]{1,0:T(8,128)(2,1)S(1)} %get-tuple-element.52), channel_id=1, source_target_pairs={{0,8},{8,0},{16,24},{24,16},{1,9},{9,1},{17,25},{25,17},{2,10},{10... | collective-permute-start | bytes 1277960 | tf_op jit(solution)/shard_map/ppermute | solution.py:608
  58.0 4.1 %shard_map.89 = (bf16[2,64,256]{2,1,0:T(8,128)(2,1)S(1)}, bf16[2,64,256]{2,1,0:T(8,128)(2,1)S(1)}, bf16[2,64,256]{2,1,0:T(8,128)(2,1)S(1)}, bf16[2,64,256]{2,1,0:T(8,128)(2,1)S(1)}) custom-call(bf16[416,512]{1,0:T(8,128)(2,1)S(1)} %get-tuple-element.51.even_ref, bf16[416,512]{1,0:T(8,128)(2,1)S(1)} %collective-permute-done.9.odd_ref), custom_call_target="tpu_custom_call" | custom-call | flops 4000000000 | bytes 1114112 | tf_op jit(solution)/shard_map/pallas_call | solution.py:26
  62.6 1.2 %collective-permute-start.14 = (bf16[2,64,256]{2,1,0:T(8,128)(2,1)S(1)}, bf16[2,64,256]{2,1,0:T(8,128)(2,1)S(1)}, u32[]{:S(2)}, u32[]{:S(2)}) collective-permute-start(bf16[2,64,256]{2,1,0:T(8,128)(2,1)S(1)} %get-tuple-element.61), channel_id=1, source_target_pairs={{0,16},{8,24},{16,0},{24,8},{1,17},{9,25},{17,1},{25,9},{2,18},{10... | collective-permute-start | bytes 196616 | tf_op jit(solution)/shard_map/ppermute | solution.py:546
  63.9 0.5 collective-permute-start.15
  64.4 1.5 %shard_map.90.rest_10_ = bf16[64,8,1024]{2,1,0:T(8,128)(2,1)} custom-call(s32[1]{0:T(128)} %bitcast.me_ref, s32[1]{0:T(128)} %bitcast.1.odd_ref, bf16[2,64,256]{2,1,0:T(8,128)(2,1)S(1)} %get-tuple-element.63.rest_0_, bf16[2,64,256]{2,1,0:T(8,128)(2,1)S(1)} %collective-permute-done.16.rest_1_, bf16[8,32,1024]{2,1,0:T(8,128)(2,1)S(1)} %get-tuple-element.57.rest_0_.rest_2_, ...), custom_call_target="tpu_custom_call" | custom-call | flops 1000000000 | bytes 7471112 | tf_op jit(solution)/shard_map/pallas_call | solution.py:526
  66.2 1.8 %collective-permute-done.15.rest_1_ = bf16[2,64,256]{2,1,0:T(8,128)(2,1)S(1)} collective-permute-done((bf16[2,64,256]{2,1,0:T(8,128)(2,1)S(1)}, bf16[2,64,256]{2,1,0:T(8,128)(2,1)S(1)}, u32[]{:S(2)}, u32[]{:S(2)}) %collective-permute-start.15) | collective-permute-done | bytes 65568 | tf_op jit(solution)/shard_map/ppermute | solution.py:546
  68.0 1.5 %shard_map.91 = bf16[64,8,1024]{2,1,0:T(8,128)(2,1)} custom-call(s32[1]{0:T(128)} %bitcast.me_ref, s32[1]{0:T(128)} %bitcast.1.odd_ref, bf16[2,64,256]{2,1,0:T(8,128)(2,1)S(1)} %collective-permute-done.14.rest_0_, bf16[2,64,256]{2,1,0:T(8,128)(2,1)S(1)} %collective-permute-done.15.rest_1_, ...), custom_call_target="tpu_custom_call", output_to_operand_aliasing={{}: (12, {})} | custom-call | flops 1000000000 | bytes 8519688 | tf_op jit(solution)/shard_map/pallas_call | solution.py:526
  (38 shorter events, 3.8 us)
Async XLA Ops:
  0.0 0.7 %copy-start.3 = (bf16[8,1024]{1,0:T(8,128)(2,1)S(1)}, bf16[8,1024]{1,0:T(8,128)(2,1)}, u32[]{:S(2)}) copy-start(bf16[8,1024]{1,0:T(8,128)(2,1)} %rest_1_.2) | copy-start | bytes 49156
  0.8 1.2 %copy-start = (bf16[64,8,1024]{2,1,0:T(8,128)(2,1)S(1)}, bf16[64,8,1024]{2,1,0:T(8,128)(2,1)}, u32[]{:S(2)}) copy-start(bf16[64,8,1024]{2,1,0:T(8,128)(2,1)} %prior_ref.3) | copy-start | bytes 3145732
  2.0 4.7 %copy-start.1 = (bf16[64,8,1024]{2,1,0:T(8,128)(2,1)S(1)}, bf16[64,8,1024]{2,1,0:T(8,128)(2,1)}, u32[]{:S(2)}) copy-start(bf16[64,8,1024]{2,1,0:T(8,128)(2,1)} %prior_ref.3) | copy-start | bytes 3145732
  2.3 14.3 %collective-permute-start = (bf16[144,1024]{1,0:T(8,128)(2,1)S(1)}, bf16[144,1024]{1,0:T(8,128)(2,1)S(1)}, u32[]{:S(2)}, u32[]{:S(2)}) collective-permute-start(bf16[144,1024]{1,0:T(8,128)(2,1)S(1)} %get-tuple-element.36.near_ref), channel_id=1, source_target_pairs={{0,1},{1,0},{2,3},{3,2},{4,5},{5,4},{6,7},{7,6},{8,9},{9,8},{10,11... | collective-permute-start | bytes 884744 | tf_op jit(solution)/shard_map/ppermute | solution.py:567
  2.6 13.9 %collective-permute-start.1 = (bf16[144,1024]{1,0:T(8,128)(2,1)S(1)}, bf16[144,1024]{1,0:T(8,128)(2,1)S(1)}, u32[]{:S(2)}, u32[]{:S(2)}) collective-permute-start(bf16[144,1024]{1,0:T(8,128)(2,1)S(1)} %get-tuple-element.37.far_ref), channel_id=1, source_target_pairs={{1,2},{3,4},{5,6},{2,1},{4,3},{6,5},{9,10},{11,12},{13,14},{10,9},... | collective-permute-start | bytes 884744 | tf_op jit(solution)/shard_map/ppermute | solution.py:567
  16.5 4.5 %copy-start.6 = (s32[1,2,128]{2,1,0:T(2,128)S(1)}, s32[1,2,128]{2,1,0:T(2,128)}, u32[]{:S(2)}) copy-start(s32[1,2,128]{2,1,0:T(2,128)} %rest_1_.3) | copy-start | bytes 3076
  16.5 4.5 %copy-start.8 = (f32[4]{0:T(128)S(1)}, f32[4]{0:T(128)}, u32[]{:S(2)}) copy-start(f32[4]{0:T(128)} %rest_3_.1) | copy-start | bytes 52
  16.5 4.5 %copy-start.5 = (f32[1,2,128]{2,1,0:T(2,128)S(1)}, f32[1,2,128]{2,1,0:T(2,128)}, u32[]{:S(2)}) copy-start(f32[1,2,128]{2,1,0:T(2,128)} %rest_0_.3) | copy-start | bytes 3076
  16.5 4.5 %copy-start.7 = (s32[1,2]{1,0:T(1,128)S(1)}, s32[1,2]{1,0:T(1,128)}, u32[]{:S(2)}) copy-start(s32[1,2]{1,0:T(1,128)} %rest_2_.1) | copy-start | bytes 28
  16.6 11.9 %collective-permute-start.2 = (bf16[128,1024]{1,0:T(8,128)(2,1)S(1)}, bf16[128,1024]{1,0:T(8,128)(2,1)S(1)}, u32[]{:S(2)}, u32[]{:S(2)}) collective-permute-start(bf16[128,1024]{1,0:T(8,128)(2,1)S(1)} %get-tuple-element.43.near_ref), channel_id=1, source_target_pairs={{0,1},{1,0},{2,3},{3,2},{4,5},{5,4},{6,7},{7,6},{8,9},{9,8},{10,11... | collective-permute-start | bytes 786440 | tf_op jit(solution)/shard_map/ppermute | solution.py:567
  16.9 11.6 %collective-permute-start.3 = (bf16[128,1024]{1,0:T(8,128)(2,1)S(1)}, bf16[128,1024]{1,0:T(8,128)(2,1)S(1)}, u32[]{:S(2)}, u32[]{:S(2)}) collective-permute-start(bf16[128,1024]{1,0:T(8,128)(2,1)S(1)} %get-tuple-element.44.far_ref), channel_id=1, source_target_pairs={{1,2},{3,4},{5,6},{2,1},{4,3},{6,5},{9,10},{11,12},{13,14},{10,9},... | collective-permute-start | bytes 786440 | tf_op jit(solution)/shard_map/ppermute | solution.py:567
  25.6 16.9 %collective-permute-start.4 = (bf16[8,32,1024]{2,1,0:T(8,128)(2,1)S(1)}, bf16[8,32,1024]{2,1,0:T(8,128)(2,1)S(1)}, u32[]{:S(2)}, u32[]{:S(2)}) collective-permute-start(bf16[8,32,1024]{2,1,0:T(8,128)(2,1)S(1)} %get-tuple-element.57.rest_0_.rest_2_), channel_id=1, source_target_pairs={{0,16},{8,24},{16,0},{24,8},{1,17},{9,25},{17,1},{25,9},{2,18},{10... | collective-permute-start | bytes 1572872 | tf_op jit(solution)/shard_map/ppermute | solution.py:554
  32.5 15.8 %collective-permute-start.5 = (bf16[8,32,1024]{2,1,0:T(8,128)(2,1)S(1)}, bf16[8,32,1024]{2,1,0:T(8,128)(2,1)S(1)}, u32[]{:S(2)}, u32[]{:S(2)}) collective-permute-start(bf16[8,32,1024]{2,1,0:T(8,128)(2,1)S(1)} %get-tuple-element.59.rest_1_.rest_6_), channel_id=1, source_target_pairs={{0,16},{8,24},{16,0},{24,8},{1,17},{9,25},{17,1},{25,9},{2,18},{10... | collective-permute-start | bytes 1572872 | tf_op jit(solution)/shard_map/ppermute | solution.py:554
  33.8 7.1 %collective-permute-start.7 = (bf16[80,1024]{1,0:T(8,128)(2,1)S(1)}, bf16[80,1024]{1,0:T(8,128)(2,1)S(1)}, u32[]{:S(2)}, u32[]{:S(2)}) collective-permute-start(bf16[80,1024]{1,0:T(8,128)(2,1)S(1)} %get-tuple-element.48.own_ref), channel_id=1, source_target_pairs={{1,2},{3,4},{5,6},{2,1},{4,3},{6,5},{9,10},{11,12},{13,14},{10,9},... | collective-permute-start | bytes 491528 | tf_op jit(solution)/shard_map/ppermute | solution.py:567
  35.8 6.3 %collective-permute-start.6 = (bf16[80,1024]{1,0:T(8,128)(2,1)S(1)}, bf16[80,1024]{1,0:T(8,128)(2,1)S(1)}, u32[]{:S(2)}, u32[]{:S(2)}) collective-permute-start(bf16[80,1024]{1,0:T(8,128)(2,1)S(1)} %get-tuple-element.48.own_ref), channel_id=1, source_target_pairs={{0,1},{1,0},{2,3},{3,2},{4,5},{5,4},{6,7},{7,6},{8,9},{9,8},{10,11... | collective-permute-start | bytes 491528 | tf_op jit(solution)/shard_map/ppermute | solution.py:567
  42.2 11.3 %collective-permute-start.8 = (bf16[2,80,768]{2,1,0:T(8,128)(2,1)S(1)}, bf16[2,80,768]{2,1,0:T(8,128)(2,1)S(1)}, u32[]{:S(2)}, u32[]{:S(2)}) collective-permute-start(bf16[2,80,768]{2,1,0:T(8,128)(2,1)S(1)} %get-tuple-element.50), channel_id=1, source_target_pairs={{0,16},{8,24},{16,0},{24,8},{1,17},{9,25},{17,1},{25,9},{2,18},{10... | collective-permute-start | bytes 737288 | tf_op jit(solution)/shard_map/ppermute | solution.py:604
  53.5 4.5 %collective-permute-start.9 = (bf16[416,512]{1,0:T(8,128)(2,1)S(1)}, bf16[416,512]{1,0:T(8,128)(2,1)S(1)}, u32[]{:S(2)}, u32[]{:S(2)}) collective-permute-start(bf16[416,512]{1,0:T(8,128)(2,1)S(1)} %get-tuple-element.52), channel_id=1, source_target_pairs={{0,8},{8,0},{16,24},{24,16},{1,9},{9,1},{17,25},{25,17},{2,10},{10... | collective-permute-start | bytes 1277960 | tf_op jit(solution)/shard_map/ppermute | solution.py:608
  56.6 5.5 %collective-permute-start.10 = (bf16[8,32,1024]{2,1,0:T(8,128)(2,1)S(1)}, bf16[8,32,1024]{2,1,0:T(8,128)(2,1)S(1)}, u32[]{:S(2)}, u32[]{:S(2)}) collective-permute-start(bf16[8,32,1024]{2,1,0:T(8,128)(2,1)S(1)} %get-tuple-element.57.rest_0_.rest_2_), channel_id=1, source_target_pairs={{0,8},{8,0},{16,24},{24,16},{1,9},{9,1},{17,25},{25,17},{2,10},{10... | collective-permute-start | bytes 1572872 | tf_op jit(solution)/shard_map/ppermute | solution.py:554
  56.7 5.4 %collective-permute-start.11 = (bf16[8,32,1024]{2,1,0:T(8,128)(2,1)S(1)}, bf16[8,32,1024]{2,1,0:T(8,128)(2,1)S(1)}, u32[]{:S(2)}, u32[]{:S(2)}) collective-permute-start(bf16[8,32,1024]{2,1,0:T(8,128)(2,1)S(1)} %collective-permute-done.4.rest_2_.rest_4_), channel_id=1, source_target_pairs={{0,8},{8,0},{16,24},{24,16},{1,9},{9,1},{17,25},{25,17},{2,10},{10... | collective-permute-start | bytes 1572872 | tf_op jit(solution)/shard_map/ppermute | solution.py:554
  57.2 5.0 %collective-permute-start.12 = (bf16[8,32,1024]{2,1,0:T(8,128)(2,1)S(1)}, bf16[8,32,1024]{2,1,0:T(8,128)(2,1)S(1)}, u32[]{:S(2)}, u32[]{:S(2)}) collective-permute-start(bf16[8,32,1024]{2,1,0:T(8,128)(2,1)S(1)} %get-tuple-element.59.rest_1_.rest_6_), channel_id=1, source_target_pairs={{0,8},{8,0},{16,24},{24,16},{1,9},{9,1},{17,25},{25,17},{2,10},{10... | collective-permute-start | bytes 1572872 | tf_op jit(solution)/shard_map/ppermute | solution.py:554
  57.2 4.9 %collective-permute-start.13 = (bf16[8,32,1024]{2,1,0:T(8,128)(2,1)S(1)}, bf16[8,32,1024]{2,1,0:T(8,128)(2,1)S(1)}, u32[]{:S(2)}, u32[]{:S(2)}) collective-permute-start(bf16[8,32,1024]{2,1,0:T(8,128)(2,1)S(1)} %collective-permute-done.5.rest_3_.rest_8_), channel_id=1, source_target_pairs={{0,8},{8,0},{16,24},{24,16},{1,9},{9,1},{17,25},{25,17},{2,10},{10... | collective-permute-start | bytes 1572872 | tf_op jit(solution)/shard_map/ppermute | solution.py:554
  62.2 2.2 %collective-permute-start.16 = (bf16[2,64,256]{2,1,0:T(8,128)(2,1)S(1)}, bf16[2,64,256]{2,1,0:T(8,128)(2,1)S(1)}, u32[]{:S(2)}, u32[]{:S(2)}) collective-permute-start(bf16[2,64,256]{2,1,0:T(8,128)(2,1)S(1)} %get-tuple-element.64), channel_id=1, source_target_pairs={{0,8},{8,0},{16,24},{24,16},{1,9},{9,1},{17,25},{25,17},{2,10},{10... | collective-permute-start | bytes 196616 | tf_op jit(solution)/shard_map/ppermute | solution.py:546
  62.6 3.6 %collective-permute-start.14 = (bf16[2,64,256]{2,1,0:T(8,128)(2,1)S(1)}, bf16[2,64,256]{2,1,0:T(8,128)(2,1)S(1)}, u32[]{:S(2)}, u32[]{:S(2)}) collective-permute-start(bf16[2,64,256]{2,1,0:T(8,128)(2,1)S(1)} %get-tuple-element.61), channel_id=1, source_target_pairs={{0,16},{8,24},{16,0},{24,8},{1,17},{9,25},{17,1},{25,9},{2,18},{10... | collective-permute-start | bytes 196616 | tf_op jit(solution)/shard_map/ppermute | solution.py:546
  63.9 4.2 %collective-permute-start.15 = (bf16[2,64,256]{2,1,0:T(8,128)(2,1)S(1)}, bf16[2,64,256]{2,1,0:T(8,128)(2,1)S(1)}, u32[]{:S(2)}, u32[]{:S(2)}) collective-permute-start(bf16[2,64,256]{2,1,0:T(8,128)(2,1)S(1)} %get-tuple-element.62), channel_id=1, source_target_pairs={{0,24},{8,16},{16,8},{24,0},{1,25},{9,17},{17,9},{25,1},{2,26},{10... | collective-permute-start | bytes 196616 | tf_op jit(solution)/shard_map/ppermute | solution.py:546
  (2 other events, 1.4 us)
